TPU v7x, 32 devices: a whole 2x2x4 slice. The times are simulated.
32 devices in a mesh: gx: 8 (over y, x, core), gy: 4 (over z).
Axes of the slice: x: 2, y: 2, z: 4, core: 2. Of those that a mesh axis runs over, the one named last changes fastest.
Arguments:
- charge_blocks: float32 [32768, 128], P(('gx', 'gy')), may hold values from -6 to 6
- block_tile: int32 [32768], P(('gx', 'gy')), may hold values from 0 to 49151, as said below
- block_count: int32 [32], P(('gx', 'gy')), may hold values from 512 to 1024, as said below
- near_kernel: float32 [9, 9, 9], replicated, may hold values from -0.21875 to 0.21875
- mid_kernel: float32 [9, 9, 9], replicated, may hold values from -0.109375 to 0.109375
- top_weights: float32 [4], replicated, may hold values from 0.0020412415 to 0.1
- top_widths: float32 [4], replicated, may hold values from 1 to 6
Outputs:
- potential: float32 [256, 96, 256], P('gx', 'gy')
Inputs may be any that keep to these rules, and one draw needn't show every extreme that they name: `block_tile`: of the 1024 slots of one device, exactly 32 name tiles in the pencil of each device, dead slots included. Slots 0 to block_count - 1 of a device are live, the others hold values that are ignored.
All inputs are finite; a program needn't handle non-finite values.
Results may differ from a plain program's by a relative error of at most 0.000082.
Values sent between devices are 32-bit elements; how exact they have to be, the bound alone decides.
A program may use at most 128 MiB of HBM per device.

v0:
```python
import jax
import jax.numpy as jnp
from jax import lax
from jax.sharding import PartitionSpec as P

CX = 32
CY = 24
NZ = 256
RADIUS = 4
ZB = 128


PRECISE = lax.Precision.HIGHEST


def extended_2(block, sides, width):
    for axis, dim in sides:
        count = lax.axis_size(axis)
        forward = [(i, i + 1) for i in range(count - 1)]
        forward.append((count - 1, 0))
        backward = [(target, source) for source, target in forward]
        low = lax.ppermute(
            lax.slice_in_dim(block, block.shape[dim] - width, None, axis=dim), axis, forward
        )
        high = lax.ppermute(lax.slice_in_dim(block, 0, width, axis=dim), axis, backward)
        block = jnp.concatenate([low, block, high], axis=dim)
    return block


def shifted(block, axis, distance):
    devices = range(lax.axis_size(axis))
    route = [((i - distance) % len(devices), i) for i in devices]
    return lax.ppermute(block, axis, route)


def band_table(width_z, radius):
    level_ids = jnp.arange(2 * radius + 1, dtype=jnp.int32)[:, None, None]
    window_ids = jnp.arange(width_z + 2 * radius, dtype=jnp.int32)[None, :, None]
    output_ids = jnp.arange(width_z, dtype=jnp.int32)[None, None, :]
    return (window_ids - output_ids == level_ids).astype(jnp.float32)


def widen(values):
    return extended_2(values, (("gx", 0), ("gy", 1)), RADIUS)


def cutoff(padded, kernel):
    diameter = 2 * RADIUS + 1
    span = ZB + 2 * RADIUS
    row_count = padded.shape[0] - 2 * RADIUS
    col_count = padded.shape[1] - 2 * RADIUS
    depth_z = padded.shape[2]
    extended = jnp.concatenate(
        [padded[:, :, depth_z - RADIUS :], padded, padded[:, :, :RADIUS]], axis=2
    )
    table = band_table(ZB, RADIUS)

    def add_shift(row_shift, running):
        slab_rows = lax.dynamic_slice_in_dim(extended, row_shift, row_count, 0)
        weights = lax.dynamic_index_in_dim(kernel, row_shift, 0, keepdims=False)
        banded = jnp.einsum("ye,ewz->ywz", weights, table, precision=PRECISE).reshape(
            diameter * span, ZB
        )
        pieces = []
        for stripe in range(depth_z // ZB):
            window = slab_rows[:, :, stripe * ZB : stripe * ZB + span]
            stacked = jnp.stack(
                [window[:, shift_y : shift_y + col_count] for shift_y in range(diameter)], axis=2
            )
            stacked = stacked.reshape(row_count * col_count, diameter * span)
            pieces.append(
                jnp.dot(stacked, banded, precision=PRECISE, preferred_element_type=jnp.float32)
            )
        return running + jnp.concatenate(pieces, axis=1)

    start_sum = jnp.zeros((row_count * col_count, depth_z), jnp.float32)
    summed = lax.fori_loop(0, diameter, add_shift, start_sum)
    return summed.reshape(row_count, col_count, depth_z)


def wrap_depth(values):
    return jnp.concatenate([values[:, :, -1:], values, values[:, :, :1]], axis=2)


def thin_out(extended, axis_dim):
    length = extended.shape[axis_dim] - 2
    centre = lax.slice_in_dim(extended, 1, length + 1, 2, axis_dim)
    before = lax.slice_in_dim(extended, 0, length, 2, axis_dim)
    behind = lax.slice_in_dim(extended, 2, length + 2, 2, axis_dim)
    return centre + 0.5 * (before + behind)


def restrict(padded):
    row_count = padded.shape[0] - 2 * RADIUS
    col_count = padded.shape[1] - 2 * RADIUS
    inner = padded[RADIUS - 1 : RADIUS + row_count + 1, RADIUS - 1 : RADIUS + col_count + 1]
    halved = thin_out(inner, 0)
    halved = thin_out(halved, 1)
    return thin_out(wrap_depth(halved), 2)


def spread_next(extended, axis_dim):
    length = extended.shape[axis_dim] - 1
    centre = lax.slice_in_dim(extended, 0, length, 1, axis_dim)
    following = lax.slice_in_dim(extended, 1, length + 1, 1, axis_dim)
    paired = jnp.stack([centre, 0.5 * (centre + following)], axis=axis_dim + 1)
    layout = list(centre.shape)
    layout[axis_dim] = 2 * length
    return paired.reshape(layout)


def prolong(values):
    upper_row = shifted(values[:1], "gx", -1)
    taller = jnp.concatenate([values, upper_row], axis=0)
    upper_col = shifted(taller[:, :1], "gy", -1)
    padded = jnp.concatenate([taller, upper_col], axis=1)
    finer = spread_next(padded, 0)
    finer = spread_next(finer, 1)
    finer = jnp.concatenate([finer, finer[:, :, :1]], axis=2)
    return spread_next(finer, 2)


def gaussians(period, widths, first_row, row_count):
    row_ids = first_row + jnp.arange(row_count, dtype=jnp.int32)[:, None]
    col_ids = jnp.arange(period, dtype=jnp.int32)[None, :]
    offset = (row_ids - col_ids) % period
    distance = jnp.minimum(offset, period - offset).astype(jnp.float32)
    return jnp.exp(-(distance * distance)[None] / (widths * widths)[:, None, None])


def top_level(top_charge, top_weights, top_widths):
    rows_x, rows_y, depth_z = top_charge.shape
    period_x = rows_x * lax.axis_size("gx")
    period_y = rows_y * lax.axis_size("gy")
    gauss_x = gaussians(period_x, top_widths, lax.axis_index("gx") * rows_x, rows_x)
    gauss_y = gaussians(period_y, top_widths, lax.axis_index("gy") * rows_y, rows_y)
    gauss_z = gaussians(depth_z, top_widths, 0, depth_z)
    column = lax.all_gather(top_charge, "gx", axis=0, tiled=True)
    partial_rows = jnp.einsum("kia,abc->kibc", gauss_x, column, precision=PRECISE)
    plane = lax.all_gather(partial_rows, "gy", axis=2, tiled=True)
    along_y = jnp.einsum("kjb,kibc->kijc", gauss_y, plane, precision=PRECISE)
    along_z = jnp.einsum("kzc,kijc->kijz", gauss_z, along_y, precision=PRECISE)
    return jnp.einsum("k,kijz->ijz", top_weights, along_z, precision=PRECISE)


def on_device(
    charge_blocks, block_tile, block_count, near_kernel, mid_kernel, top_weights, top_widths
):
    size_x = lax.axis_size("gx")
    size_y = lax.axis_size("gy")
    device_total = size_x * size_y
    slot_total = charge_blocks.shape[0]
    per_owner = slot_total // device_total
    stripes = NZ // ZB
    grid_y = CY * size_y
    live_slot = jnp.arange(slot_total, dtype=jnp.int32) < block_count[0]
    masked = charge_blocks * live_slot[:, None].astype(jnp.float32)
    column_ids = block_tile // stripes
    stripe_ids = block_tile % stripes
    global_x = column_ids // grid_y
    global_y = column_ids % grid_y
    owner_ids = global_x // CX * size_y + global_y // CY
    local_tile = (global_x % CX * CY + global_y % CY) * stripes + stripe_ids
    ordering = jnp.argsort(owner_ids, stable=True)
    outgoing = masked[ordering].reshape(size_x, size_y, per_owner, ZB)
    outgoing_ids = local_tile[ordering].reshape(size_x, size_y, per_owner)
    arrived, arrived_ids = (
        lax.all_to_all(
            outgoing.reshape(device_total, per_owner, ZB),
            ("gx", "gy"),
            split_axis=0,
            concat_axis=0,
            tiled=True,
        ),
        lax.all_to_all(
            outgoing_ids.reshape(device_total, per_owner),
            ("gx", "gy"),
            split_axis=0,
            concat_axis=0,
            tiled=True,
        ),
    )
    fine_charge = jax.ops.segment_sum(
        arrived.reshape(-1, ZB), arrived_ids.reshape(-1), num_segments=CX * CY * stripes
    )
    fine_charge = fine_charge.reshape(CX, CY, NZ)
    fine_padded = widen(fine_charge)
    mid_charge = restrict(fine_padded)
    mid_padded = widen(mid_charge)
    top_charge = restrict(mid_padded)
    top_potential = top_level(top_charge, top_weights, top_widths)
    mid_potential = cutoff(mid_padded, mid_kernel) + prolong(top_potential)
    return cutoff(fine_padded, near_kernel) + prolong(mid_potential)


def solution(mesh):
    placed = (P(("gx", "gy"), None), P(("gx", "gy")), P(("gx", "gy")), P(), P(), P(), P())
    return jax.shard_map(
        on_device, mesh=mesh, in_specs=placed, out_specs=P("gx", "gy", None), check_vma=False
    )
```

profile of v0, /device:TPU:0, one launch (start us, length us, event | category | flops | bytes accessed | tf_op | source)
XLA Modules:
  0.0 884.3 jit_solution(10794743002061156892)
XLA Ops:
  29.7 13.1 %all-to-all-done.1 = f32[32,32,128]{2,1,0:T(8,128)S(1)} async-done(((f32[32,32,128]{2,1,0:T(8,128)}), f32[32,32,128]{2,1,0:T(8,128)S(1)}, u32[]{:S(2)}, u32[]{:S(2)}) %all-to-all-start.1) | async-done | bytes 524320 | tf_op jit(solution)/shard_map/all_to_all | solution.py:168
  95.9 9.4 %all_gather.6 = f32[64,6,64]{2,0,1:T(8,128)S(1)} all-gather(f32[8,6,64]{2,0,1:T(8,128)S(1)} %multiply_add_fusion.4), channel_id=1, replica_groups=mesh['gx'=8,'gy'=4] {'gx'}, dimensions={0}, use_global_device_ids=true | all-gather | bytes 110592 | tf_op jit(solution)/shard_map/all_gather | solution.py:138
  105.6 15.3 %all_gather.7 = f32[4,8,24,64]{3,1,2,0:T(8,128)S(1)} all-gather(f32[4,8,6,64]{3,1,2,0:T(8,128)S(1)} %fusion.51), channel_id=1, replica_groups=mesh['gx'=8,'gy'=4] {'gy'}, dimensions={2}, use_global_device_ids=true | all-gather | bytes 245760 | tf_op jit(solution)/shard_map/all_gather | solution.py:140
  127.5 107.4 %while.29 = (s32[]{:T(128)}, f32[192,128]{1,0:T(8,128)S(1)}, f32[24,20,136]{2,0,1:T(8,128)S(1)}, f32[9,9,9]{2,1,0:T(8,128)}, s32[136,128]{1,0:T(8,128)S(1)}, /*i...) while((s32[]{:T(128)}, f32[192,128]{1,0:T(8,128)S(1)}, ...), condition=%wide.region_5.6_spmd.clone, body=%wide.region_4.5_spmd.clone.sunk | while | flops 378255360 | bytes 13398811 | solution.py:77
  241.8 633.7 %while.28 = (s32[]{:T(128)}, f32[768,256]{0,1:T(8,128)}, f32[40,32,264]{2,0,1:T(8,128)S(1)}, f32[9,9,9]{2,1,0:T(8,128)}, s32[136,128]{1,0:T(8,128)S(1)}, /*index...) while((s32[]{:T(128)}, f32[768,256]{0,1:T(8,128)}, ...), condition=%wide.region_3.4_spmd.clone, body=%wide.region_2.3_spmd.clone.sunk | while | flops 2905602048 | bytes 116654952 | solution.py:77
  285.9 10.2 %reshape.264 = f32[768,1224]{1,0:T(8,128)} reshape(f32[32,24,9,136]{3,2,1,0:T(8,128)} %copy.242) | data formatting | bytes 7520256 | tf_op jit(solution)/shard_map/while/body/eval_jaxpr/reshape | solution.py:70
  303.8 9.0 %copy.240 = f32[32,24,9,136]{3,2,1,0:T(8,128)} copy(f32[32,24,9,136]{3,1,0,2:T(8,128)S(1)} %copy-done.3) | data formatting | bytes 7520256 | tf_op jit(solution)/shard_map/while/body/eval_jaxpr/stack | solution.py:67
  312.8 10.2 %reshape.263 = f32[768,1224]{1,0:T(8,128)} reshape(f32[32,24,9,136]{3,2,1,0:T(8,128)} %copy.240) | data formatting | bytes 7520256 | tf_op jit(solution)/shard_map/while/body/eval_jaxpr/reshape | solution.py:70
  353.0 10.2 %reshape.264 = f32[768,1224]{1,0:T(8,128)} reshape(f32[32,24,9,136]{3,2,1,0:T(8,128)} %copy.242) | data formatting | bytes 7520256 | tf_op jit(solution)/shard_map/while/body/eval_jaxpr/reshape | solution.py:70
  370.9 9.0 %copy.240 = f32[32,24,9,136]{3,2,1,0:T(8,128)} copy(f32[32,24,9,136]{3,1,0,2:T(8,128)S(1)} %copy-done.3) | data formatting | bytes 7520256 | tf_op jit(solution)/shard_map/while/body/eval_jaxpr/stack | solution.py:67
  379.9 10.2 %reshape.263 = f32[768,1224]{1,0:T(8,128)} reshape(f32[32,24,9,136]{3,2,1,0:T(8,128)} %copy.240) | data formatting | bytes 7520256 | tf_op jit(solution)/shard_map/while/body/eval_jaxpr/reshape | solution.py:70
  421.2 10.2 %reshape.264 = f32[768,1224]{1,0:T(8,128)} reshape(f32[32,24,9,136]{3,2,1,0:T(8,128)} %copy.242) | data formatting | bytes 7520256 | tf_op jit(solution)/shard_map/while/body/eval_jaxpr/reshape | solution.py:70
  439.2 9.0 %copy.240 = f32[32,24,9,136]{3,2,1,0:T(8,128)} copy(f32[32,24,9,136]{3,1,0,2:T(8,128)S(1)} %copy-done.3) | data formatting | bytes 7520256 | tf_op jit(solution)/shard_map/while/body/eval_jaxpr/stack | solution.py:67
  448.1 10.2 %reshape.263 = f32[768,1224]{1,0:T(8,128)} reshape(f32[32,24,9,136]{3,2,1,0:T(8,128)} %copy.240) | data formatting | bytes 7520256 | tf_op jit(solution)/shard_map/while/body/eval_jaxpr/reshape | solution.py:70
  489.5 10.2 %reshape.264 = f32[768,1224]{1,0:T(8,128)} reshape(f32[32,24,9,136]{3,2,1,0:T(8,128)} %copy.242) | data formatting | bytes 7520256 | tf_op jit(solution)/shard_map/while/body/eval_jaxpr/reshape | solution.py:70
  507.4 9.0 %copy.240 = f32[32,24,9,136]{3,2,1,0:T(8,128)} copy(f32[32,24,9,136]{3,1,0,2:T(8,128)S(1)} %copy-done.3) | data formatting | bytes 7520256 | tf_op jit(solution)/shard_map/while/body/eval_jaxpr/stack | solution.py:67
  516.4 10.2 %reshape.263 = f32[768,1224]{1,0:T(8,128)} reshape(f32[32,24,9,136]{3,2,1,0:T(8,128)} %copy.240) | data formatting | bytes 7520256 | tf_op jit(solution)/shard_map/while/body/eval_jaxpr/reshape | solution.py:70
  557.7 10.2 %reshape.264 = f32[768,1224]{1,0:T(8,128)} reshape(f32[32,24,9,136]{3,2,1,0:T(8,128)} %copy.242) | data formatting | bytes 7520256 | tf_op jit(solution)/shard_map/while/body/eval_jaxpr/reshape | solution.py:70
  575.7 9.0 %copy.240 = f32[32,24,9,136]{3,2,1,0:T(8,128)} copy(f32[32,24,9,136]{3,1,0,2:T(8,128)S(1)} %copy-done.3) | data formatting | bytes 7520256 | tf_op jit(solution)/shard_map/while/body/eval_jaxpr/stack | solution.py:67
  584.6 10.2 %reshape.263 = f32[768,1224]{1,0:T(8,128)} reshape(f32[32,24,9,136]{3,2,1,0:T(8,128)} %copy.240) | data formatting | bytes 7520256 | tf_op jit(solution)/shard_map/while/body/eval_jaxpr/reshape | solution.py:70
  626.0 10.2 %reshape.264 = f32[768,1224]{1,0:T(8,128)} reshape(f32[32,24,9,136]{3,2,1,0:T(8,128)} %copy.242) | data formatting | bytes 7520256 | tf_op jit(solution)/shard_map/while/body/eval_jaxpr/reshape | solution.py:70
  643.9 9.0 %copy.240 = f32[32,24,9,136]{3,2,1,0:T(8,128)} copy(f32[32,24,9,136]{3,1,0,2:T(8,128)S(1)} %copy-done.3) | data formatting | bytes 7520256 | tf_op jit(solution)/shard_map/while/body/eval_jaxpr/stack | solution.py:67
  652.9 10.2 %reshape.263 = f32[768,1224]{1,0:T(8,128)} reshape(f32[32,24,9,136]{3,2,1,0:T(8,128)} %copy.240) | data formatting | bytes 7520256 | tf_op jit(solution)/shard_map/while/body/eval_jaxpr/reshape | solution.py:70
  694.2 10.2 %reshape.264 = f32[768,1224]{1,0:T(8,128)} reshape(f32[32,24,9,136]{3,2,1,0:T(8,128)} %copy.242) | data formatting | bytes 7520256 | tf_op jit(solution)/shard_map/while/body/eval_jaxpr/reshape | solution.py:70
  712.2 9.0 %copy.240 = f32[32,24,9,136]{3,2,1,0:T(8,128)} copy(f32[32,24,9,136]{3,1,0,2:T(8,128)S(1)} %copy-done.3) | data formatting | bytes 7520256 | tf_op jit(solution)/shard_map/while/body/eval_jaxpr/stack | solution.py:67
  721.1 10.2 %reshape.263 = f32[768,1224]{1,0:T(8,128)} reshape(f32[32,24,9,136]{3,2,1,0:T(8,128)} %copy.240) | data formatting | bytes 7520256 | tf_op jit(solution)/shard_map/while/body/eval_jaxpr/reshape | solution.py:70
  762.5 10.2 %reshape.264 = f32[768,1224]{1,0:T(8,128)} reshape(f32[32,24,9,136]{3,2,1,0:T(8,128)} %copy.242) | data formatting | bytes 7520256 | tf_op jit(solution)/shard_map/while/body/eval_jaxpr/reshape | solution.py:70
  780.4 9.0 %copy.240 = f32[32,24,9,136]{3,2,1,0:T(8,128)} copy(f32[32,24,9,136]{3,1,0,2:T(8,128)S(1)} %copy-done.3) | data formatting | bytes 7520256 | tf_op jit(solution)/shard_map/while/body/eval_jaxpr/stack | solution.py:67
  789.4 10.2 %reshape.263 = f32[768,1224]{1,0:T(8,128)} reshape(f32[32,24,9,136]{3,2,1,0:T(8,128)} %copy.240) | data formatting | bytes 7520256 | tf_op jit(solution)/shard_map/while/body/eval_jaxpr/reshape | solution.py:70
  830.7 10.2 %reshape.264 = f32[768,1224]{1,0:T(8,128)} reshape(f32[32,24,9,136]{3,2,1,0:T(8,128)} %copy.242) | data formatting | bytes 7520256 | tf_op jit(solution)/shard_map/while/body/eval_jaxpr/reshape | solution.py:70
  848.6 9.0 %copy.240 = f32[32,24,9,136]{3,2,1,0:T(8,128)} copy(f32[32,24,9,136]{3,1,0,2:T(8,128)S(1)} %copy-done.3) | data formatting | bytes 7520256 | tf_op jit(solution)/shard_map/while/body/eval_jaxpr/stack | solution.py:67
  857.5 10.2 %reshape.263 = f32[768,1224]{1,0:T(8,128)} reshape(f32[32,24,9,136]{3,2,1,0:T(8,128)} %copy.240) | data formatting | bytes 7520256 | tf_op jit(solution)/shard_map/while/body/eval_jaxpr/reshape | solution.py:70
  (535 shorter events, 557.2 us)
Async XLA Ops:
  0.0 121.7 %copy-start = (f32[4]{0:T(128)S(1)}, f32[4]{0:T(128)}, u32[]{:S(2)}) copy-start(f32[4]{0:T(128)} %param.16) | copy-start | bytes 52
  0.0 18.3 %copy-start.12 = (f32[1024,128]{1,0:T(8,128)S(1)}, f32[1024,128]{1,0:T(8,128)}, u32[]{:S(2)}) copy-start(f32[1024,128]{1,0:T(8,128)} %param.11) | copy-start | bytes 1572868
  10.4 14.5 %all-to-all-start = ((s32[32,1,32]{2,1,0:T(1,128)}), s32[32,1,32]{2,1,0:T(1,128)S(1)}, u32[]{:S(2)}, u32[]{:S(2)}) async-start(s32[32,1,32]{2,1,0:T(1,128)} %all_to_all.9), calls=%async_computation | async-start | bytes 32768 | tf_op jit(solution)/shard_map/all_to_all | solution.py:175
  24.9 18.0 %all-to-all-start.1 = ((f32[32,32,128]{2,1,0:T(8,128)}), f32[32,32,128]{2,1,0:T(8,128)S(1)}, u32[]{:S(2)}, u32[]{:S(2)}) async-start(f32[32,32,128]{2,1,0:T(8,128)} %bitcast.1), calls=%async_computation.1 | async-start | bytes 1048576 | tf_op jit(solution)/shard_map/all_to_all | solution.py:168
  49.2 5.0 collective-permute-start
  50.4 3.8 collective-permute-start.1
  52.5 16.4 %copy-start.4 = (f32[32,24,256]{2,0,1:T(8,128)}, f32[32,24,256]{2,0,1:T(8,128)S(1)}, u32[]{:S(2)}) copy-start(f32[32,24,256]{2,0,1:T(8,128)S(1)} %copy.53) | copy-start | bytes 2359300
  54.2 14.7 %copy-start.7 = (f32[4,24,256]{2,0,1:T(4,128)}, f32[4,24,256]{2,0,1:T(4,128)S(1)}, u32[]{:S(2)}) copy-start(f32[4,24,256]{2,0,1:T(4,128)S(1)} %collective-permute-done.1) | copy-start | bytes 294916
  54.3 9.0 %collective-permute-start.2 = (f32[40,4,256]{2,0,1:T(8,128)S(1)}, f32[40,4,256]{2,0,1:T(8,128)S(1)}, u32[]{:S(2)}, u32[]{:S(2)}) collective-permute-start(f32[40,4,256]{2,0,1:T(8,128)S(1)} %get-tuple-element.310), channel_id=1, source_target_pairs={{0,1},{1,2},{2,3},{3,0},{4,5},{5,6},{6,7},{7,4},{8,9},{9,10},{10,1... | collective-permute-start | bytes 491528 | tf_op jit(solution)/shard_map/ppermute | solution.py:22
  57.6 8.9 %collective-permute-start.3 = (f32[40,4,256]{2,0,1:T(8,128)S(1)}, f32[40,4,256]{2,0,1:T(8,128)S(1)}, u32[]{:S(2)}, u32[]{:S(2)}) collective-permute-start(f32[40,4,256]{2,0,1:T(8,128)S(1)} %get-tuple-element.311), channel_id=1, source_target_pairs={{1,0},{2,1},{3,2},{0,3},{5,4},{6,5},{7,6},{4,7},{9,8},{10,9},{11,1... | collective-permute-start | bytes 491528 | tf_op jit(solution)/shard_map/ppermute | solution.py:25
  68.9 17.4 %copy-start.14 = (f32[4]{0:T(128)S(1)}, f32[4]{0:T(128)}, u32[]{:S(2)}) copy-start(f32[4]{0:T(128)} %param.17) | copy-start | bytes 52
  83.6 4.2 collective-permute-start.4
  83.7 4.2 collective-permute-start.5
  87.8 6.1 collective-permute-start.6
  88.5 5.5 collective-permute-start.7
  122.1 1.4 collective-permute-start.8
  123.4 111.6 %collective-permute-start.9 = (f32[9,1,64]{2,0,1:T(8,128)S(1)}, f32[9,1,64]{2,0,1:T(8,128)S(1)}, u32[]{:S(2)}, u32[]{:S(2)}) collective-permute-start(f32[9,1,64]{2,0,1:T(8,128)S(1)} %pad_maximum_fusion.23), channel_id=1, source_target_pairs={{1,0},{2,1},{3,2},{0,3},{5,4},{6,5},{7,6},{4,7},{9,8},{10,9},{11,1... | collective-permute-start | bytes 6920 | tf_op jit(solution)/shard_map/ppermute | solution.py:33
  235.0 3.6 copy-start.5
  235.0 3.6 copy-start.8
  235.0 3.6 copy-start.10
  236.1 5.6 copy-start.6
  236.2 4.7 collective-permute-start.10
  241.4 635.4 %collective-permute-start.11 = (f32[17,1,128]{2,1,0:T(1,128)}, f32[17,1,128]{2,1,0:T(1,128)}, u32[]{:S(2)}, u32[]{:S(2)}) collective-permute-start(f32[17,1,128]{2,1,0:T(1,128)} %pad_maximum_fusion.22), channel_id=1, source_target_pairs={{1,0},{2,1},{3,2},{0,3},{5,4},{6,5},{7,6},{4,7},{9,8},{10,9},{11,1... | collective-permute-start | bytes 26120 | tf_op jit(solution)/shard_map/ppermute | solution.py:33
  296.1 7.7 copy-start.3
  363.2 7.7 copy-start.3
  431.5 7.7 copy-start.3
  499.7 7.7 copy-start.3
  568.0 7.7 copy-start.3
  636.2 7.7 copy-start.3
  704.5 7.7 copy-start.3
  772.7 7.7 copy-start.3
  840.9 7.7 copy-start.3
  (13 other events, 33.6 us)
where the time goes:
time: 892 us; the launch traced here: 884 us
  local copies, waits for them, and re-layouts  584 us (65%)
  matrix products  153 us (17%)
  other arithmetic  38.2 us (4%)
  starting transfers between devices  31.1 us (3%)
  waiting for transfers between devices  28.6 us (3%)
  blocking collectives  24.7 us (3%)
  loops' own time  23.1 us (3%)
    reshape x27, local copies, waits for them, and re-layouts, add_shift(): stacked = stacked.reshape(row_count * col_count, diameter * span)  207 us
    another operation x45, local copies, waits for them, and re-layouts, add_shift(): jnp.stack([window[:, shift_y:shift_y + col_count] for shift_y in range(di...  198 us
    dot_general x27, matrix products, add_shift(): jnp.dot(stacked, banded, precision=PRECISE, preferred_element_type=jnp.fl...  118 us
    while x252, local copies, waits for them, and re-layouts  100 us
    dot_general x18, matrix products, add_shift(): jnp.einsum('ye,ewz->ywz', weights, table, precision=PRECISE)  33.1 us
    slice x18, local copies, waits for them, and re-layouts, add_shift(): window[:, shift_y:shift_y + col_count]  32.5 us
    another operation x2, loops' own time, cutoff(): summed = lax.fori_loop(0, diameter, add_shift, start_sum)  23.1 us
    add x9, other arithmetic, add_shift(): return running + jnp.concatenate(pieces, axis=1)  18 us
  transfers between devices with their start and end apart: 14, of which 8 were waited for; matrix products, arithmetic and copies ran while one was open for 80% of the time, Pallas kernels for 0%

commit v1 on v0

v1 whole, which is shorter than its diff:
```python
import functools

import jax
import jax.numpy as jnp
from jax import lax
from jax.experimental import pallas as pl
from jax.experimental.pallas import tpu as pltpu
from jax.sharding import PartitionSpec as P

CX = 32
CY = 24
NZ = 256
RADIUS = 4
ZB = 128
DIAM = 2 * RADIUS + 1
IDROWS = 8


PRECISE = lax.Precision.HIGHEST
BF = jnp.bfloat16
F32 = jnp.float32
VMEM = pl.BlockSpec(memory_space=pltpu.VMEM)
SMEM = pl.BlockSpec(memory_space=pltpu.SMEM)


def params(mib):
    return pltpu.CompilerParams(vmem_limit_bytes=mib * 2**20)


def split2(values):
    high = values.astype(BF)
    low = (values - high.astype(F32)).astype(BF)
    return high, low


def split3(values):
    high = values.astype(BF)
    rest = values - high.astype(F32)
    mid = rest.astype(BF)
    return high, mid, (rest - mid.astype(F32)).astype(BF)


def mm(a, b):
    return jnp.dot(a, b, preferred_element_type=F32)


def iota(shape, dim):
    return lax.broadcasted_iota(jnp.int32, shape, dim)


def dispatch_kernel(devices, count_ref, owner_ref, tile_ref, charge_ref, out_ref, parts_ref):
    slots = charge_ref.shape[0]
    per_owner = slots // devices
    chunk = 512
    live = iota((slots, ZB), 0) < count_ref[0]
    high, mid, low = split3(jnp.where(live, charge_ref[...], 0.0))
    parts_ref[:, :ZB] = high
    parts_ref[:, ZB : 2 * ZB] = mid
    parts_ref[:, 2 * ZB :] = low
    upper = (iota((chunk, chunk), 0) < iota((chunk, chunk), 1)).astype(F32).astype(BF)
    before = jnp.zeros((devices, 1), F32)
    ranks = []
    tiles = jnp.zeros((devices, ZB), F32)
    for part in range(slots // chunk):
        lanes = slice(part * chunk, (part + 1) * chunk)
        owned = iota((devices, chunk), 0) == owner_ref[:, lanes]
        owned_f = owned.astype(F32)
        earlier = mm(owned_f.astype(BF), upper) + before
        before = before + jnp.sum(owned_f, axis=1, keepdims=True)
        rank = jnp.sum(jnp.where(owned, earlier, 0.0), axis=0, keepdims=True).astype(jnp.int32)
        ranks.append(rank)
        places = (iota((ZB, chunk), 0) == rank).astype(F32).astype(BF)
        ids = tile_ref[:, lanes]
        coarse = lax.shift_right_logical(ids, 6).astype(F32)
        fine = (ids & 63).astype(F32)
        across = (((1,), (1,)), ((), ()))
        for factor, value in ((64.0, coarse), (1.0, fine)):
            tiles = tiles + factor * lax.dot_general(
                (owned_f * value).astype(BF), places, across, preferred_element_type=F32
            )
    position = owner_ref[...] * per_owner + jnp.concatenate(ranks, axis=1)
    group = 256 // per_owner
    rows = group * per_owner

    def place(step, carry):
        chosen = (iota((rows, slots), 0) + step * rows == position).astype(F32).astype(BF)
        picked = mm(chosen, parts_ref[...])
        total = picked[:, :ZB] + (picked[:, ZB : 2 * ZB] + picked[:, 2 * ZB :])
        out_ref[pl.ds(step * group, group), :per_owner, :] = total.reshape(group, per_owner, ZB)
        return carry

    lax.fori_loop(0, devices // group, place, 0)
    out_ref[:, per_owner:, :] = jnp.broadcast_to(tiles[:, None, :], (devices, IDROWS, ZB))


def gather_kernel(ids_ref, arrived_ref, out_ref, parts_ref):
    devices, rows, _ = arrived_ref.shape
    per_owner = rows - IDROWS
    slots = devices * per_owner
    high, mid, low = split3(arrived_ref[:, :per_owner, :].reshape(slots, ZB))
    parts_ref[:, :ZB] = high
    parts_ref[:, ZB : 2 * ZB] = mid
    parts_ref[:, 2 * ZB :] = low
    tall = 8

    def add(step, carry):
        for stripe in range(NZ // ZB):
            first = stripe * CX * CY + step * tall * CX
            chosen = (iota((tall * CX, slots), 0) + first == ids_ref[...]).astype(F32).astype(BF)
            picked = mm(chosen, parts_ref[...])
            total = picked[:, :ZB] + (picked[:, ZB : 2 * ZB] + picked[:, 2 * ZB :])
            out_ref[pl.ds(step * tall, tall), :, stripe * ZB : (stripe + 1) * ZB] = total.reshape(
                tall, CX, ZB
            )
        return carry

    lax.fori_loop(0, CY // tall, add, 0)


def cutoff_kernel(tall, kernel_ref, padded_ref, out_ref, high_ref, low_ref, wide_ref, thin_ref):
    rows_y, rows_x, depth = out_ref.shape
    for a in range(DIAM):
        high, low = split2(padded_ref[:, a : a + rows_x, :])
        high_ref[:, :, a * depth : (a + 1) * depth] = high
        low_ref[:, :, a * depth : (a + 1) * depth] = low
    offset = iota((16, depth), 0) - iota((16, depth), 1) + RADIUS
    offset = jnp.where(offset < 0, offset + depth, offset)

    def shift(b, carry):
        for a in range(DIAM):
            base = jnp.zeros((16, depth), F32)
            for e in range(DIAM):
                base = jnp.where(offset == e, kernel_ref[(a * DIAM + b) * DIAM + e], base)
            base_high = base.astype(BF).astype(F32)
            base_low = base - base_high
            for i in range(depth // 16):
                at = slice(a * depth + 16 * i, a * depth + 16 * i + 16)
                wide_ref[at, :] = (pltpu.roll(base_high, 16 * i, 1) if i else base_high).astype(BF)
                thin_ref[at, :] = (pltpu.roll(base_low, 16 * i, 1) if i else base_low).astype(BF)

        def block(step, inner):
            at = pl.ds(step * tall + b, tall)
            high = high_ref[at].reshape(tall * rows_x, DIAM * depth)
            low = low_ref[at].reshape(tall * rows_x, DIAM * depth)
            part = mm(high, wide_ref[...]) + (mm(high, thin_ref[...]) + mm(low, wide_ref[...]))
            here = pl.ds(step * tall, tall)
            part = part.reshape(tall, rows_x, depth)

            @pl.when(b == 0)
            def _():
                out_ref[here] = part

            @pl.when(b > 0)
            def _():
                out_ref[here] += part

            return inner

        return lax.fori_loop(0, rows_y // tall, block, carry)

    lax.fori_loop(0, DIAM, shift, 0)


def cutoff(padded, kernel, tall):
    rows_y, rows_x, depth = padded.shape
    rows_y, rows_x = rows_y - 2 * RADIUS, rows_x - 2 * RADIUS
    wide = DIAM * depth
    return pl.pallas_call(
        functools.partial(cutoff_kernel, tall),
        out_shape=jax.ShapeDtypeStruct((rows_y, rows_x, depth), F32),
        in_specs=[SMEM, VMEM],
        out_specs=VMEM,
        scratch_shapes=[
            pltpu.VMEM((rows_y + 2 * RADIUS, rows_x, wide), BF),
            pltpu.VMEM((rows_y + 2 * RADIUS, rows_x, wide), BF),
            pltpu.VMEM((wide, depth), BF),
            pltpu.VMEM((wide, depth), BF),
        ],
        compiler_params=params(40),
        cost_estimate=pl.CostEstimate(
            flops=6 * rows_y * rows_x * depth * depth * DIAM * DIAM,
            bytes_accessed=8 * rows_y * rows_x * depth,
            transcendentals=0,
        ),
    )(kernel.reshape(-1), padded)


def extended_2(block, sides, width):
    for axis, dim in sides:
        count = lax.axis_size(axis)
        forward = [(i, i + 1) for i in range(count - 1)]
        forward.append((count - 1, 0))
        backward = [(target, source) for source, target in forward]
        low = lax.ppermute(
            lax.slice_in_dim(block, block.shape[dim] - width, None, axis=dim), axis, forward
        )
        high = lax.ppermute(lax.slice_in_dim(block, 0, width, axis=dim), axis, backward)
        block = jnp.concatenate([low, block, high], axis=dim)
    return block


def shifted(block, axis, distance):
    devices = range(lax.axis_size(axis))
    route = [((i - distance) % len(devices), i) for i in devices]
    return lax.ppermute(block, axis, route)


def widen(values):
    return extended_2(values, (("gx", 1), ("gy", 0)), RADIUS)


def wrap_depth(values):
    return jnp.concatenate([values[:, :, -1:], values, values[:, :, :1]], axis=2)


def thin_out(extended, axis_dim):
    length = extended.shape[axis_dim] - 2
    centre = lax.slice_in_dim(extended, 1, length + 1, 2, axis_dim)
    before = lax.slice_in_dim(extended, 0, length, 2, axis_dim)
    behind = lax.slice_in_dim(extended, 2, length + 2, 2, axis_dim)
    return centre + 0.5 * (before + behind)


def restrict(padded):
    row_count = padded.shape[0] - 2 * RADIUS
    col_count = padded.shape[1] - 2 * RADIUS
    inner = padded[RADIUS - 1 : RADIUS + row_count + 1, RADIUS - 1 : RADIUS + col_count + 1]
    halved = thin_out(inner, 0)
    halved = thin_out(halved, 1)
    return thin_out(wrap_depth(halved), 2)


def spread_next(extended, axis_dim):
    length = extended.shape[axis_dim] - 1
    centre = lax.slice_in_dim(extended, 0, length, 1, axis_dim)
    following = lax.slice_in_dim(extended, 1, length + 1, 1, axis_dim)
    paired = jnp.stack([centre, 0.5 * (centre + following)], axis=axis_dim + 1)
    layout = list(centre.shape)
    layout[axis_dim] = 2 * length
    return paired.reshape(layout)


def prolong(values):
    upper_row = shifted(values[:, :1], "gx", -1)
    taller = jnp.concatenate([values, upper_row], axis=1)
    upper_col = shifted(taller[:1], "gy", -1)
    padded = jnp.concatenate([taller, upper_col], axis=0)
    finer = spread_next(padded, 0)
    finer = spread_next(finer, 1)
    finer = jnp.concatenate([finer, finer[:, :, :1]], axis=2)
    return spread_next(finer, 2)


def gaussians(period, widths, first_row, row_count):
    row_ids = first_row + jnp.arange(row_count, dtype=jnp.int32)[:, None]
    col_ids = jnp.arange(period, dtype=jnp.int32)[None, :]
    offset = (row_ids - col_ids) % period
    distance = jnp.minimum(offset, period - offset).astype(jnp.float32)
    return jnp.exp(-(distance * distance)[None] / (widths * widths)[:, None, None])


def top_level(top_charge, top_weights, top_widths):
    rows_y, rows_x, depth_z = top_charge.shape
    period_x = rows_x * lax.axis_size("gx")
    period_y = rows_y * lax.axis_size("gy")
    gauss_x = gaussians(period_x, top_widths, lax.axis_index("gx") * rows_x, rows_x)
    gauss_y = gaussians(period_y, top_widths, lax.axis_index("gy") * rows_y, rows_y)
    gauss_z = gaussians(depth_z, top_widths, 0, depth_z)
    column = lax.all_gather(top_charge, "gx", axis=1, tiled=True)
    partial_rows = jnp.einsum("kia,bac->kbic", gauss_x, column, precision=PRECISE)
    plane = lax.all_gather(partial_rows, "gy", axis=1, tiled=True)
    along_y = jnp.einsum("kjb,kbic->kjic", gauss_y, plane, precision=PRECISE)
    along_z = jnp.einsum("kzc,kjic->kjiz", gauss_z, along_y, precision=PRECISE)
    return jnp.einsum("k,kjiz->jiz", top_weights, along_z, precision=PRECISE)


def fine_charges(charge_blocks, block_tile, block_count):
    size_x = lax.axis_size("gx")
    size_y = lax.axis_size("gy")
    device_total = size_x * size_y
    slot_total = charge_blocks.shape[0]
    per_owner = slot_total // device_total
    stripes = NZ // ZB
    grid_y = CY * size_y
    column_ids = block_tile // stripes
    stripe_ids = block_tile % stripes
    global_x = column_ids // grid_y
    global_y = column_ids % grid_y
    owner_ids = global_x // CX * size_y + global_y // CY
    local_tile = (stripe_ids * CY + global_y % CY) * CX + global_x % CX
    outgoing = pl.pallas_call(
        functools.partial(dispatch_kernel, device_total),
        out_shape=jax.ShapeDtypeStruct((device_total, per_owner + IDROWS, ZB), F32),
        in_specs=[SMEM, VMEM, VMEM, VMEM],
        out_specs=VMEM,
        scratch_shapes=[pltpu.VMEM((slot_total, 3 * ZB), BF)],
        compiler_params=params(40),
    )(block_count, owner_ids.reshape(1, -1), local_tile.reshape(1, -1), charge_blocks)
    arrived = lax.all_to_all(outgoing, ("gx", "gy"), split_axis=0, concat_axis=0, tiled=True)
    ids = arrived[:, per_owner, :per_owner].astype(jnp.int32).reshape(1, slot_total)
    return pl.pallas_call(
        gather_kernel,
        out_shape=jax.ShapeDtypeStruct((CY, CX, NZ), F32),
        in_specs=[VMEM, VMEM],
        out_specs=VMEM,
        scratch_shapes=[pltpu.VMEM((slot_total, 3 * ZB), BF)],
        compiler_params=params(40),
    )(ids, arrived)


def on_device(
    charge_blocks, block_tile, block_count, near_kernel, mid_kernel, top_weights, top_widths
):
    fine_charge = fine_charges(charge_blocks, block_tile, block_count)
    fine_padded = widen(fine_charge)
    mid_charge = restrict(fine_padded)
    mid_padded = widen(mid_charge)
    top_charge = restrict(mid_padded)
    top_potential = top_level(top_charge, top_weights, top_widths)
    mid_potential = cutoff(mid_padded, mid_kernel, 12) + prolong(top_potential)
    potential = cutoff(fine_padded, near_kernel, 8) + prolong(mid_potential)
    return jnp.transpose(potential, (1, 0, 2))


def solution(mesh):
    placed = (P(("gx", "gy"), None), P(("gx", "gy")), P(("gx", "gy")), P(), P(), P(), P())
    return jax.shard_map(
        on_device, mesh=mesh, in_specs=placed, out_specs=P("gx", "gy", None), check_vma=False
    )
```

time: 892 us -> 161 us (0.18)
  local copies, waits for them, and re-layouts: 584 us -> 20.3 us
  matrix products: 153 us -> 1.54 us
  Pallas kernels: 0 us -> 49.2 us
  other arithmetic: 38.2 us -> 2.52 us
  loops' own time: 23.1 us -> 0 us
    reshape x30 -> x2, local copies, waits for them, and re-layouts: 207 us -> 0.29 us  [cutoff(): kernel.reshape(-1)]
    another operation x46 -> x0, local copies, waits for them, and re-layouts: 198 us -> none  [the longest x45 198 us: add_shift(): jnp.stack([window[:, shift_y:shift_y + col_count] for shift_y in range(di...]
    dot_general x49 -> x4, matrix products: 153 us -> 1.54 us  [the longest x1 0.53 us: top_level(): along_y = jnp.einsum('kjb,kbic->kjic', gauss_y, plane, precision=PRECISE)]
    while x253 -> x0, local copies, waits for them, and re-layouts: 102 us -> none
    pallas_call x0 -> x4, Pallas kernels: none -> 49.2 us  [the longest x2 43.5 us: cutoff(): pl.pallas_call(functools.partial(cutoff_kernel, tall), out_shape=jax.Shap...]
    slice x24 -> x2, local copies, waits for them, and re-layouts: 33.9 us -> 0.01 us  [prolong(): upper_row = shifted(values[:, :1], 'gx', -1)]
    another operation x2 -> x0, loops' own time: 23.1 us -> none  [cutoff(): summed = lax.fori_loop(0, diameter, add_shift, start_sum)]
    add x12 -> x2, other arithmetic: 19.8 us -> 0.74 us  [the longest x1 0.72 us: fine_charges(): local_tile = (stripe_ids * CY + global_y % CY) * CX + global_x % CX]
  transfers between devices with their start and end apart: 14 -> 13, of which waited for: 8 -> 8; matrix products, arithmetic and copies ran while one was open for 80% -> 0% of each run, Pallas kernels for 0% -> 27%
where the time goes in v1:
time: 161 us; the launch traced here: 160 us
  Pallas kernels  49.2 us (31%)
  waiting for transfers between devices  33.6 us (21%)
  starting transfers between devices  27.3 us (17%)
  blocking collectives  24.6 us (15%)
  local copies, waits for them, and re-layouts  20.3 us (13%)
  other arithmetic  2.52 us (2%)
    pallas_call x2, Pallas kernels, cutoff(): pl.pallas_call(functools.partial(cutoff_kernel, tall), out_shape=jax.Shap...  43.5 us
    all_to_all x1, waiting for transfers between devices, fine_charges(): lax.all_to_all(outgoing, ('gx', 'gy'), split_axis=0, concat_axis=0, tiled...  16.9 us
    all_gather x1, blocking collectives, top_level(): plane = lax.all_gather(partial_rows, 'gy', axis=1, tiled=True)  15 us
    ppermute x4, waiting for transfers between devices, extended_2(): lax.ppermute(lax.slice_in_dim(block, block.shape[dim] - width, None, axis...  11 us
    all_gather x1, blocking collectives, top_level(): column = lax.all_gather(top_charge, 'gx', axis=1, tiled=True)  9.51 us
    all_to_all x1, starting transfers between devices, fine_charges(): lax.all_to_all(outgoing, ('gx', 'gy'), split_axis=0, concat_axis=0, tiled...  7.3 us
    ppermute x4, starting transfers between devices, extended_2(): lax.ppermute(lax.slice_in_dim(block, 0, width, axis=dim), axis, backward)  7.12 us
    ppermute x4, starting transfers between devices, shifted(): return lax.ppermute(block, axis, route)  6.83 us
  transfers between devices with their start and end apart: 13, of which 8 were waited for; matrix products, arithmetic and copies ran while one was open for 0% of the time, Pallas kernels for 27%

profile of v1, /device:TPU:0, one launch (start us, length us, event | category | flops | bytes accessed | tf_op | source)
XLA Modules:
  0.0 160.2 jit_solution(130706302858353010)
XLA Ops:
  0.7 0.7 fusion.51
  1.4 1.0 copy-done.1
  2.4 3.4 %shard_map.73 = f32[32,40,128]{2,1,0:T(8,128)} custom-call(s32[1]{0:T(128)S(6)} %copy.63.count_ref, s32[1,1024]{1,0:T(1,128)S(1)} %bitcast.64, s32[1,1024]{1,0:T(1,128)S(1)} %bitcast.63, f32[1024,128]{1,0:T(8,128)S(1)} %copy-done.1), custom_call_target="tpu_custom_call" | custom-call | tf_op jit(solution)/shard_map/pallas_call | solution.py:291
  5.9 7.3 %all-to-all-start = ((f32[32,40,128]{2,1,0:T(8,128)}), f32[32,40,128]{2,1,0:T(8,128)S(1)}, u32[]{:S(2)}, u32[]{:S(2)}) async-start(f32[32,40,128]{2,1,0:T(8,128)} %shard_map.73), calls=%async_computation | async-start | bytes 1310720 | tf_op jit(solution)/shard_map/all_to_all | solution.py:299
  13.2 16.9 %all-to-all-done.arrived_ref = f32[32,40,128]{2,1,0:T(8,128)S(1)} async-done(((f32[32,40,128]{2,1,0:T(8,128)}), f32[32,40,128]{2,1,0:T(8,128)S(1)}, u32[]{:S(2)}, u32[]{:S(2)}) %all-to-all-start) | async-done | bytes 655392 | tf_op jit(solution)/shard_map/all_to_all | solution.py:299
  30.2 2.3 %shard_map.74 = f32[24,32,256]{2,1,0:T(8,128)S(1)} custom-call(s32[1,1024]{1,0:T(1,128)S(1)} %convert_element_type.35.ids_ref, f32[32,40,128]{2,1,0:T(8,128)S(1)} %all-to-all-done.arrived_ref), custom_call_target="tpu_custom_call" | custom-call | tf_op jit(solution)/shard_map/pallas_call | solution.py:301
  32.6 1.4 collective-permute-start
  34.0 1.3 collective-permute-start.1
  35.3 2.3 %collective-permute-done = f32[24,4,256]{2,1,0:T(4,128)S(1)} collective-permute-done((f32[24,4,256]{2,1,0:T(4,128)S(1)}, f32[24,4,256]{2,1,0:T(4,128)S(1)}, u32[]{:S(2)}, u32[]{:S(2)}) %collective-permute-start) | collective-permute-done | bytes 98336 | tf_op jit(solution)/shard_map/ppermute | solution.py:194
  37.6 3.9 %collective-permute-start.2 = (f32[4,40,256]{2,1,0:T(8,128)S(1)}, f32[4,40,256]{2,1,0:T(8,128)S(1)}, u32[]{:S(2)}, u32[]{:S(2)}) collective-permute-start(f32[4,40,256]{2,1,0:T(8,128)S(1)} %get-tuple-element.5), channel_id=1, source_target_pairs={{0,1},{1,2},{2,3},{3,0},{4,5},{5,6},{6,7},{7,4},{8,9},{9,10},{10,1... | collective-permute-start | bytes 491528 | tf_op jit(solution)/shard_map/ppermute | solution.py:194
  41.6 5.1 %collective-permute-done.2 = f32[4,40,256]{2,1,0:T(8,128)S(1)} collective-permute-done((f32[4,40,256]{2,1,0:T(8,128)S(1)}, f32[4,40,256]{2,1,0:T(8,128)S(1)}, u32[]{:S(2)}, u32[]{:S(2)}) %collective-permute-start.2) | collective-permute-done | bytes 163872 | tf_op jit(solution)/shard_map/ppermute | solution.py:194
  46.7 3.4 %collective-permute-done.3 = f32[4,40,256]{2,1,0:T(8,128)S(1)} collective-permute-done((f32[4,40,256]{2,1,0:T(8,128)S(1)}, f32[4,40,256]{2,1,0:T(8,128)S(1)}, u32[]{:S(2)}, u32[]{:S(2)}) %collective-permute-start.3) | collective-permute-done | bytes 163872 | tf_op jit(solution)/shard_map/ppermute | solution.py:197
  50.9 3.3 %slice.153 = f32[12,16,128]{2,1,0:T(8,128)S(1)} slice(f32[12,16,256]{2,1,0:T(8,128)S(1)} %multiply_add_fusion.1), slice={[0:12:1], [0:16:1], [0:256:2]} | slice | bytes 196608 | tf_op jit(solution)/shard_map/slice | solution.py:218
  54.4 3.3 %slice.157 = f32[12,16,128]{2,1,0:T(8,128)S(1)} slice(f32[12,16,258]{2,1,0:T(8,128)S(1)} %pad_maximum_fusion.4), slice={[0:12:1], [0:16:1], [2:258:2]} | slice | bytes 196608 | tf_op jit(solution)/shard_map/slice | solution.py:220
  57.7 3.3 %slice.156 = f32[12,16,128]{2,1,0:T(8,128)S(1)} slice(f32[12,16,258]{2,1,0:T(8,128)S(1)} %pad_maximum_fusion.4), slice={[0:12:1], [0:16:1], [0:256:2]} | slice | bytes 196608 | tf_op jit(solution)/shard_map/slice | solution.py:219
  61.1 2.6 %collective-permute-start.5 = (f32[12,4,128]{2,1,0:T(4,128)S(1)}, f32[12,4,128]{2,1,0:T(4,128)S(1)}, u32[]{:S(2)}, u32[]{:S(2)}) collective-permute-start(f32[12,4,128]{2,1,0:T(4,128)S(1)} %get-tuple-element.20), channel_id=1, source_target_pairs={{4,0},{8,4},{12,8},{16,12},{20,16},{24,20},{28,24},{0,28},{5,1},{9... | collective-permute-start | bytes 73736 | tf_op jit(solution)/shard_map/ppermute | solution.py:197
  63.8 1.4 collective-permute-done.4
  65.3 0.6 collective-permute-start.6
  65.9 3.2 %collective-permute-start.7 = (f32[4,24,128]{2,1,0:T(8,128)S(1)}, f32[4,24,128]{2,1,0:T(8,128)S(1)}, u32[]{:S(2)}, u32[]{:S(2)}) collective-permute-start(f32[4,24,128]{2,1,0:T(8,128)S(1)} %get-tuple-element.14), channel_id=1, source_target_pairs={{1,0},{2,1},{3,2},{0,3},{5,4},{6,5},{7,6},{4,7},{9,8},{10,9},{11,1... | collective-permute-start | bytes 147464 | tf_op jit(solution)/shard_map/ppermute | solution.py:197
  69.2 2.2 %collective-permute-done.6 = f32[4,24,128]{2,1,0:T(8,128)S(1)} collective-permute-done((f32[4,24,128]{2,1,0:T(8,128)S(1)}, f32[4,24,128]{2,1,0:T(8,128)S(1)}, u32[]{:S(2)}, u32[]{:S(2)}) %collective-permute-start.6) | collective-permute-done | bytes 49184 | tf_op jit(solution)/shard_map/ppermute | solution.py:194
  73.2 9.5 %all_gather.6 = f32[6,64,64]{2,1,0:T(8,128)S(1)} all-gather(f32[6,8,64]{2,1,0:T(8,128)S(1)} %multiply_add_fusion.4), channel_id=1, replica_groups=mesh['gx'=8,'gy'=4] {'gx'}, dimensions={1}, use_global_device_ids=true | all-gather | bytes 110592 | tf_op jit(solution)/shard_map/all_gather | solution.py:269
  83.0 15.0 %all_gather.7 = f32[4,24,8,64]{3,2,0,1:T(8,128)S(1)} all-gather(f32[4,6,8,64]{3,2,0,1:T(8,128)S(1)} %convolution_bitcast_fusion), channel_id=1, replica_groups=mesh['gx'=8,'gy'=4] {'gy'}, dimensions={1}, use_global_device_ids=true | all-gather | bytes 245760 | tf_op jit(solution)/shard_map/all_gather | solution.py:271
  98.0 0.5 fusion.3
  99.6 1.1 collective-permute-done.8
  100.7 4.1 %collective-permute-start.9 = (f32[1,9,64]{2,1,0:T(8,128)S(1)}, f32[1,9,64]{2,1,0:T(8,128)S(1)}, u32[]{:S(2)}, u32[]{:S(2)}) collective-permute-start(f32[1,9,64]{2,1,0:T(8,128)S(1)} %fusion.41), channel_id=1, source_target_pairs={{1,0},{2,1},{3,2},{0,3},{5,4},{6,5},{7,6},{4,7},{9,8},{10,9},{11,1... | collective-permute-start | bytes 6920 | tf_op jit(solution)/shard_map/ppermute | solution.py:205
  104.8 6.6 %shard_map.76 = f32[12,16,128]{2,1,0:T(8,128)S(1)} custom-call(f32[729]{0:T(1024)S(1)} %reshape.152.kernel_ref, f32[20,24,128]{2,1,0:T(8,128)S(1)} %pad_maximum_fusion.6.padded_ref), custom_call_target="tpu_custom_call" | custom-call | flops 1528823808 | bytes 196608 | tf_op jit(solution)/shard_map/pallas_call | solution.py:168
  112.5 2.4 %collective-permute-start.10 = (f32[12,1,128]{2,1,0:T(1,128)S(1)}, f32[12,1,128]{2,1,0:T(1,128)S(1)}, u32[]{:S(2)}, u32[]{:S(2)}) collective-permute-start(f32[12,1,128]{2,1,0:T(1,128)S(1)} %slice.205), channel_id=1, source_target_pairs={{4,0},{8,4},{12,8},{16,12},{20,16},{24,20},{28,24},{0,28},{5,1},{9... | collective-permute-start | bytes 18440 | tf_op jit(solution)/shard_map/ppermute | solution.py:205
  115.1 1.2 collective-permute-done.10
  116.6 36.9 %shard_map.75 = f32[24,32,256]{2,1,0:T(8,128)S(1)} custom-call(f32[729]{0:T(1024)S(1)} %reshape.149.kernel_ref, f32[32,40,256]{2,1,0:T(8,128)S(1)} %pad_maximum_fusion.padded_ref), custom_call_target="tpu_custom_call" | custom-call | flops 24461180928 | bytes 1572864 | tf_op jit(solution)/shard_map/pallas_call | solution.py:168
  154.1 2.3 %copy.47 = f32[24,32,128,2]{1,0,3,2:T(8,128)} copy(f32[24,32,128,2]{2,0,1,3:T(8,128)S(1)} %pad_maximum_fusion.1) | data formatting | bytes 1572864 | tf_op jit(solution)/shard_map/stack | solution.py:237
  156.4 2.3 %copy.48 = f32[24,32,256]{2,1,0:T(8,128)S(1)} copy(f32[24,32,256]{1,0,2:T(8,128)} %bitcast.65) | data formatting | bytes 1572864 | tf_op jit(solution)/shard_map/reshape | solution.py:240
  158.9 1.3 copy.49
  (80 shorter events, 6.7 us)
Async XLA Ops:
  0.0 99.0 %copy-start = (f32[4]{0:T(128)S(1)}, f32[4]{0:T(128)}, u32[]{:S(2)}) copy-start(f32[4]{0:T(128)} %param.12) | copy-start | bytes 52
  1.4 1.0 copy-start.1
  5.9 24.2 %all-to-all-start = ((f32[32,40,128]{2,1,0:T(8,128)}), f32[32,40,128]{2,1,0:T(8,128)S(1)}, u32[]{:S(2)}, u32[]{:S(2)}) async-start(f32[32,40,128]{2,1,0:T(8,128)} %shard_map.73), calls=%async_computation | async-start | bytes 1310720 | tf_op jit(solution)/shard_map/all_to_all | solution.py:299
  32.6 5.0 %collective-permute-start = (f32[24,4,256]{2,1,0:T(4,128)S(1)}, f32[24,4,256]{2,1,0:T(4,128)S(1)}, u32[]{:S(2)}, u32[]{:S(2)}) collective-permute-start(f32[24,4,256]{2,1,0:T(4,128)S(1)} %get-tuple-element.7), channel_id=1, source_target_pairs={{0,4},{4,8},{8,12},{12,16},{16,20},{20,24},{24,28},{28,0},{1,5},{5... | collective-permute-start | bytes 294920 | tf_op jit(solution)/shard_map/ppermute | solution.py:194
  34.0 3.5 %collective-permute-start.1 = (f32[24,4,256]{2,1,0:T(4,128)S(1)}, f32[24,4,256]{2,1,0:T(4,128)S(1)}, u32[]{:S(2)}, u32[]{:S(2)}) collective-permute-start(f32[24,4,256]{2,1,0:T(4,128)S(1)} %get-tuple-element.8), channel_id=1, source_target_pairs={{4,0},{8,4},{12,8},{16,12},{20,16},{24,20},{28,24},{0,28},{5,1},{9... | collective-permute-start | bytes 294920 | tf_op jit(solution)/shard_map/ppermute | solution.py:197
  37.6 9.1 %collective-permute-start.2 = (f32[4,40,256]{2,1,0:T(8,128)S(1)}, f32[4,40,256]{2,1,0:T(8,128)S(1)}, u32[]{:S(2)}, u32[]{:S(2)}) collective-permute-start(f32[4,40,256]{2,1,0:T(8,128)S(1)} %get-tuple-element.5), channel_id=1, source_target_pairs={{0,1},{1,2},{2,3},{3,0},{4,5},{5,6},{6,7},{7,4},{8,9},{9,10},{10,1... | collective-permute-start | bytes 491528 | tf_op jit(solution)/shard_map/ppermute | solution.py:194
  41.5 8.5 %collective-permute-start.3 = (f32[4,40,256]{2,1,0:T(8,128)S(1)}, f32[4,40,256]{2,1,0:T(8,128)S(1)}, u32[]{:S(2)}, u32[]{:S(2)}) collective-permute-start(f32[4,40,256]{2,1,0:T(8,128)S(1)} %get-tuple-element.6), channel_id=1, source_target_pairs={{1,0},{2,1},{3,2},{0,3},{5,4},{6,5},{7,6},{4,7},{9,8},{10,9},{11,1... | collective-permute-start | bytes 491528 | tf_op jit(solution)/shard_map/ppermute | solution.py:197
  50.9 18.4 %copy-start.4 = (f32[4]{0:T(128)S(1)}, f32[4]{0:T(128)}, u32[]{:S(2)}) copy-start(f32[4]{0:T(128)} %param.13) | copy-start | bytes 52
  61.1 4.2 %collective-permute-start.4 = (f32[12,4,128]{2,1,0:T(4,128)S(1)}, f32[12,4,128]{2,1,0:T(4,128)S(1)}, u32[]{:S(2)}, u32[]{:S(2)}) collective-permute-start(f32[12,4,128]{2,1,0:T(4,128)S(1)} %get-tuple-element.19), channel_id=1, source_target_pairs={{0,4},{4,8},{8,12},{12,16},{16,20},{20,24},{24,28},{28,0},{1,5},{5... | collective-permute-start | bytes 73736 | tf_op jit(solution)/shard_map/ppermute | solution.py:194
  61.1 4.2 %collective-permute-start.5 = (f32[12,4,128]{2,1,0:T(4,128)S(1)}, f32[12,4,128]{2,1,0:T(4,128)S(1)}, u32[]{:S(2)}, u32[]{:S(2)}) collective-permute-start(f32[12,4,128]{2,1,0:T(4,128)S(1)} %get-tuple-element.20), channel_id=1, source_target_pairs={{4,0},{8,4},{12,8},{16,12},{20,16},{24,20},{28,24},{0,28},{5,1},{9... | collective-permute-start | bytes 73736 | tf_op jit(solution)/shard_map/ppermute | solution.py:197
  65.3 6.1 %collective-permute-start.6 = (f32[4,24,128]{2,1,0:T(8,128)S(1)}, f32[4,24,128]{2,1,0:T(8,128)S(1)}, u32[]{:S(2)}, u32[]{:S(2)}) collective-permute-start(f32[4,24,128]{2,1,0:T(8,128)S(1)} %get-tuple-element.13), channel_id=1, source_target_pairs={{0,1},{1,2},{2,3},{3,0},{4,5},{5,6},{6,7},{7,4},{8,9},{9,10},{10,1... | collective-permute-start | bytes 147464 | tf_op jit(solution)/shard_map/ppermute | solution.py:194
  65.9 5.5 %collective-permute-start.7 = (f32[4,24,128]{2,1,0:T(8,128)S(1)}, f32[4,24,128]{2,1,0:T(8,128)S(1)}, u32[]{:S(2)}, u32[]{:S(2)}) collective-permute-start(f32[4,24,128]{2,1,0:T(8,128)S(1)} %get-tuple-element.14), channel_id=1, source_target_pairs={{1,0},{2,1},{3,2},{0,3},{5,4},{6,5},{7,6},{4,7},{9,8},{10,9},{11,1... | collective-permute-start | bytes 147464 | tf_op jit(solution)/shard_map/ppermute | solution.py:197
  72.0 27.4 %copy-start.2 = (f32[9,9,9]{2,1,0:T(8,128)S(1)}, f32[9,9,9]{2,1,0:T(8,128)}, u32[]{:S(2)}) copy-start(f32[9,9,9]{2,1,0:T(8,128)} %param.11) | copy-start | bytes 8752
  99.3 1.4 collective-permute-start.8
  100.7 10.7 %collective-permute-start.9 = (f32[1,9,64]{2,1,0:T(8,128)S(1)}, f32[1,9,64]{2,1,0:T(8,128)S(1)}, u32[]{:S(2)}, u32[]{:S(2)}) collective-permute-start(f32[1,9,64]{2,1,0:T(8,128)S(1)} %fusion.41), channel_id=1, source_target_pairs={{1,0},{2,1},{3,2},{0,3},{5,4},{6,5},{7,6},{4,7},{9,8},{10,9},{11,1... | collective-permute-start | bytes 6920 | tf_op jit(solution)/shard_map/ppermute | solution.py:205
  111.7 3.2 %copy-start.3 = (f32[9,9,9]{2,1,0:T(8,128)S(1)}, f32[9,9,9]{2,1,0:T(8,128)}, u32[]{:S(2)}) copy-start(f32[9,9,9]{2,1,0:T(8,128)} %param.10) | copy-start | bytes 8752
  112.5 3.7 %collective-permute-start.10 = (f32[12,1,128]{2,1,0:T(1,128)S(1)}, f32[12,1,128]{2,1,0:T(1,128)S(1)}, u32[]{:S(2)}, u32[]{:S(2)}) collective-permute-start(f32[12,1,128]{2,1,0:T(1,128)S(1)} %slice.205), channel_id=1, source_target_pairs={{4,0},{8,4},{12,8},{16,12},{20,16},{24,20},{28,24},{0,28},{5,1},{9... | collective-permute-start | bytes 18440 | tf_op jit(solution)/shard_map/ppermute | solution.py:205
  116.3 37.2 %collective-permute-start.11 = (f32[1,17,128]{2,1,0:T(8,128)S(1)}, f32[1,17,128]{2,1,0:T(8,128)S(1)}, u32[]{:S(2)}, u32[]{:S(2)}) collective-permute-start(f32[1,17,128]{2,1,0:T(8,128)S(1)} %fusion.40), channel_id=1, source_target_pairs={{1,0},{2,1},{3,2},{0,3},{5,4},{6,5},{7,6},{4,7},{9,8},{10,9},{11,1... | collective-permute-start | bytes 26120 | tf_op jit(solution)/shard_map/ppermute | solution.py:205

commit v2 on v1

--- a/solution.py
+++ b/solution.py
@@ -185,93 +185,117 @@
     )(kernel.reshape(-1), padded)
 
 
-def extended_2(block, sides, width):
-    for axis, dim in sides:
+def extended_2(block, low_width, high_width):
+    for axis, dim in (("gx", 1), ("gy", 0)):
         count = lax.axis_size(axis)
-        forward = [(i, i + 1) for i in range(count - 1)]
-        forward.append((count - 1, 0))
+        forward = [(i, (i + 1) % count) for i in range(count)]
         backward = [(target, source) for source, target in forward]
         low = lax.ppermute(
-            lax.slice_in_dim(block, block.shape[dim] - width, None, axis=dim), axis, forward
+            lax.slice_in_dim(block, block.shape[dim] - low_width, None, axis=dim), axis, forward
         )
-        high = lax.ppermute(lax.slice_in_dim(block, 0, width, axis=dim), axis, backward)
+        high = lax.ppermute(lax.slice_in_dim(block, 0, high_width, axis=dim), axis, backward)
         block = jnp.concatenate([low, block, high], axis=dim)
     return block
 
 
-def shifted(block, axis, distance):
-    devices = range(lax.axis_size(axis))
-    route = [((i - distance) % len(devices), i) for i in devices]
-    return lax.ppermute(block, axis, route)
-
-
-def widen(values):
-    return extended_2(values, (("gx", 1), ("gy", 0)), RADIUS)
-
-
-def wrap_depth(values):
-    return jnp.concatenate([values[:, :, -1:], values, values[:, :, :1]], axis=2)
-
-
-def thin_out(extended, axis_dim):
-    length = extended.shape[axis_dim] - 2
-    centre = lax.slice_in_dim(extended, 1, length + 1, 2, axis_dim)
-    before = lax.slice_in_dim(extended, 0, length, 2, axis_dim)
-    behind = lax.slice_in_dim(extended, 2, length + 2, 2, axis_dim)
-    return centre + 0.5 * (before + behind)
-
-
-def restrict(padded):
-    row_count = padded.shape[0] - 2 * RADIUS
-    col_count = padded.shape[1] - 2 * RADIUS
-    inner = padded[RADIUS - 1 : RADIUS + row_count + 1, RADIUS - 1 : RADIUS + col_count + 1]
-    halved = thin_out(inner, 0)
-    halved = thin_out(halved, 1)
-    return thin_out(wrap_depth(halved), 2)
-
-
-def spread_next(extended, axis_dim):
-    length = extended.shape[axis_dim] - 1
-    centre = lax.slice_in_dim(extended, 0, length, 1, axis_dim)
-    following = lax.slice_in_dim(extended, 1, length + 1, 1, axis_dim)
-    paired = jnp.stack([centre, 0.5 * (centre + following)], axis=axis_dim + 1)
-    layout = list(centre.shape)
-    layout[axis_dim] = 2 * length
-    return paired.reshape(layout)
-
-
-def prolong(values):
-    upper_row = shifted(values[:, :1], "gx", -1)
-    taller = jnp.concatenate([values, upper_row], axis=1)
-    upper_col = shifted(taller[:1], "gy", -1)
-    padded = jnp.concatenate([taller, upper_col], axis=0)
-    finer = spread_next(padded, 0)
-    finer = spread_next(finer, 1)
-    finer = jnp.concatenate([finer, finer[:, :, :1]], axis=2)
-    return spread_next(finer, 2)
-
-
-def gaussians(period, widths, first_row, row_count):
-    row_ids = first_row + jnp.arange(row_count, dtype=jnp.int32)[:, None]
-    col_ids = jnp.arange(period, dtype=jnp.int32)[None, :]
-    offset = (row_ids - col_ids) % period
-    distance = jnp.minimum(offset, period - offset).astype(jnp.float32)
-    return jnp.exp(-(distance * distance)[None] / (widths * widths)[:, None, None])
-
-
-def top_level(top_charge, top_weights, top_widths):
-    rows_y, rows_x, depth_z = top_charge.shape
-    period_x = rows_x * lax.axis_size("gx")
-    period_y = rows_y * lax.axis_size("gy")
-    gauss_x = gaussians(period_x, top_widths, lax.axis_index("gx") * rows_x, rows_x)
-    gauss_y = gaussians(period_y, top_widths, lax.axis_index("gy") * rows_y, rows_y)
-    gauss_z = gaussians(depth_z, top_widths, 0, depth_z)
-    column = lax.all_gather(top_charge, "gx", axis=1, tiled=True)
-    partial_rows = jnp.einsum("kia,bac->kbic", gauss_x, column, precision=PRECISE)
-    plane = lax.all_gather(partial_rows, "gy", axis=1, tiled=True)
-    along_y = jnp.einsum("kjb,kbic->kjic", gauss_y, plane, precision=PRECISE)
-    along_z = jnp.einsum("kzc,kjic->kjiz", gauss_z, along_y, precision=PRECISE)
-    return jnp.einsum("k,kjiz->jiz", top_weights, along_z, precision=PRECISE)
+def hat(distance):
+    near = jnp.where(jnp.abs(distance) == 1, 0.5, 0.0)
+    return jnp.where(distance == 0, 1.0, near)
+
+
+def hat_periodic(shape, fine_dim):
+    period = shape[fine_dim]
+    distance = iota(shape, fine_dim) - 2 * iota(shape, 1 - fine_dim)
+    distance = jnp.where(distance == 1 - period, 1, distance)
+    distance = jnp.where(distance == period - 1, 1, distance)
+    return hat(distance).astype(BF)
+
+
+def exact_left(weights, values):
+    high, mid, low = split3(values)
+    return mm(weights, high) + (mm(weights, mid) + mm(weights, low))
+
+
+def exact_right(values, weights):
+    high, mid, low = split3(values)
+    return mm(high, weights) + (mm(mid, weights) + mm(low, weights))
+
+
+def restrict_kernel(padded_ref, out_ref):
+    rows_y, rows_x, depth = out_ref.shape
+    shape = (rows_x, padded_ref.shape[1])
+    across = hat(iota(shape, 1) - RADIUS - 2 * iota(shape, 0)).astype(BF)
+    lines = []
+    for j in range(rows_y):
+        centre = RADIUS + 2 * j
+        line = padded_ref[centre] + 0.5 * (padded_ref[centre - 1] + padded_ref[centre + 1])
+        lines.append(exact_left(across, line))
+    along = hat_periodic((2 * depth, depth), 0)
+    result = exact_right(jnp.concatenate(lines, axis=0), along)
+    out_ref[...] = result.reshape(rows_y, rows_x, depth)
+
+
+def restrict(padded, rows_y, rows_x):
+    return pl.pallas_call(
+        restrict_kernel,
+        out_shape=jax.ShapeDtypeStruct((rows_y, rows_x, padded.shape[2] // 2), F32),
+        in_specs=[VMEM],
+        out_specs=VMEM,
+        compiler_params=params(32),
+    )(padded)
+
+
+def hat_plane(rows, row_bits, cols, col_bits):
+    row, col = iota((rows, cols), 0), iota((rows, cols), 1)
+    step_y = lax.shift_right_logical(row, row_bits) - 2 * lax.shift_right_logical(col, col_bits)
+    step_x = (row & (2**row_bits - 1)) - 2 * (col & (2**col_bits - 1))
+    return (hat(step_y) * hat(step_x)).astype(BF)
+
+
+def finish_kernel(plane_ref, along_ref, top_ref, mid_ref, fine_ref, out_ref):
+    devices, top_y, top_x, depth = top_ref.shape
+    top = top_ref[...].reshape(devices * top_y * top_x, depth)
+    rows = plane_ref.shape[1]
+    potential = jnp.zeros((rows, depth), F32)
+    for k in range(plane_ref.shape[0]):
+        term = jnp.dot(plane_ref[k], top, precision=PRECISE, preferred_element_type=F32)
+        potential += jnp.dot(term, along_ref[k], precision=PRECISE, preferred_element_type=F32)
+    mid_y, mid_x, mid_z = mid_ref.shape
+    mid_rows = mid_y * mid_x
+    coarse = exact_left(hat_plane(mid_rows, 5, rows, 4), potential)
+    coarse = exact_right(coarse, hat_periodic((depth, mid_z), 1))
+    middle = mid_ref[...].reshape(mid_rows, mid_z) + coarse
+    fine_y, fine_x, fine_z = fine_ref.shape
+    along = hat_periodic((mid_z, fine_z), 1)
+    middle = exact_right(middle, along)
+    finer = exact_left(hat_plane(fine_y * fine_x, 5, mid_rows, 5), middle)
+    finer = finer.reshape(fine_y, fine_x, fine_z)
+    for y in range(fine_y):
+        out_ref[:, y, :] = fine_ref[y] + finer[y]
+
+
+def wrapped(offset, period):
+    offset = offset % period
+    distance = jnp.minimum(offset, period - offset).astype(F32)
+    return distance * distance
+
+
+def top_tables(top_weights, top_widths):
+    size_x, size_y = lax.axis_size("gx"), lax.axis_size("gy")
+    top_x, top_y, depth = CX // 4, CY // 4, NZ // 4
+    cols = jnp.arange(size_x * size_y * top_x * top_y, dtype=jnp.int32)
+    owner = cols // (top_x * top_y)
+    col_x = owner // size_y * top_x + cols % top_x
+    col_y = owner % size_y * top_y + cols // top_x % top_y
+    rows = jnp.arange((top_y + 1) * 16, dtype=jnp.int32)
+    row_x = lax.axis_index("gx") * top_x + rows % 16
+    row_y = lax.axis_index("gy") * top_y + rows // 16
+    squares = wrapped(row_x[:, None] - col_x[None, :], size_x * top_x)
+    squares = squares + wrapped(row_y[:, None] - col_y[None, :], size_y * top_y)
+    widths = (top_widths * top_widths)[:, None, None]
+    line = jnp.arange(depth, dtype=jnp.int32)
+    along = jnp.exp(-wrapped(line[:, None] - line[None, :], depth)[None] / widths)
+    return jnp.exp(-squares[None] / widths), top_weights[:, None, None] * along
 
 
 def fine_charges(charge_blocks, block_tile, block_count):
@@ -312,14 +336,23 @@
     charge_blocks, block_tile, block_count, near_kernel, mid_kernel, top_weights, top_widths
 ):
     fine_charge = fine_charges(charge_blocks, block_tile, block_count)
-    fine_padded = widen(fine_charge)
-    mid_charge = restrict(fine_padded)
-    mid_padded = widen(mid_charge)
-    top_charge = restrict(mid_padded)
-    top_potential = top_level(top_charge, top_weights, top_widths)
-    mid_potential = cutoff(mid_padded, mid_kernel, 12) + prolong(top_potential)
-    potential = cutoff(fine_padded, near_kernel, 8) + prolong(mid_potential)
-    return jnp.transpose(potential, (1, 0, 2))
+    plane, along = top_tables(top_weights, top_widths)
+    fine_padded = extended_2(fine_charge, RADIUS, RADIUS)
+    mid_charge = restrict(fine_padded, CY // 2, CX // 2)
+    mid_padded = extended_2(mid_charge, RADIUS, RADIUS + 1)
+    spare = CX + 2 * RADIUS - mid_padded.shape[1]
+    mid_padded = jnp.pad(mid_padded, ((0, 0), (0, spare), (0, 0)))
+    top_charge = restrict(mid_padded, CY // 4, CX // 4)
+    top_all = lax.all_gather(top_charge, ("gx", "gy"), axis=0, tiled=False)
+    mid_cut = cutoff(mid_padded, mid_kernel, CY // 2 + 1)
+    fine_cut = cutoff(fine_padded, near_kernel, 8)
+    return pl.pallas_call(
+        finish_kernel,
+        out_shape=jax.ShapeDtypeStruct((CX, CY, NZ), F32),
+        in_specs=[VMEM] * 5,
+        out_specs=VMEM,
+        compiler_params=params(48),
+    )(plane, along, top_all, mid_cut, fine_cut)
 
 
 def solution(mesh):

time: 161 us -> 188 us (1.17)
  blocking collectives: 24.6 us -> 72.3 us
  local copies, waits for them, and re-layouts: 20.3 us -> 3.88 us
  Pallas kernels: 49.2 us -> 60.2 us
  starting transfers between devices: 27.3 us -> 20.5 us
  waiting for transfers between devices: 33.6 us -> 27.5 us
    all_gather x2 -> x1, blocking collectives: 24.6 us -> 72.3 us  [on_device(): top_all = lax.all_gather(top_charge, ('gx', 'gy'), axis=0, tiled=False)]
    slice x20 -> x3, local copies, waits for them, and re-layouts: 12 us -> 0.05 us  [the longest x2 0.04 us: extended_2(): lax.slice_in_dim(block, block.shape[dim] - low_width, None, axis=dim)]
    pallas_call x0 -> x3, Pallas kernels: none -> 6.99 us  [the longest x1 6.2 us: on_device(): pl.pallas_call(finish_kernel, out_shape=jax.ShapeDtypeStruct((CX, CY, NZ)...]
    ppermute x12 -> x8, starting transfers between devices: 20 us -> 13.2 us  [the longest x4 7.32 us: extended_2(): lax.ppermute(lax.slice_in_dim(block, 0, high_width, axis=dim), axis, back...]
    ppermute x12 -> x8, waiting for transfers between devices: 16.7 us -> 10.7 us  [the longest x4 7.06 us: extended_2(): lax.ppermute(lax.slice_in_dim(block, block.shape[dim] - low_width, None,...]
    pallas_call x2, Pallas kernels: 43.5 us -> 47.5 us  [cutoff(): pl.pallas_call(functools.partial(cutoff_kernel, tall), out_shape=jax.Shap...]
    another operation x4 -> x0, local copies, waits for them, and re-layouts: 2.96 us -> none  [spread_next(): paired = jnp.stack([centre, 0.5 * (centre + following)], axis=axis_dim + 1)]
    reshape x2 -> x0, local copies, waits for them, and re-layouts: 2.55 us -> none  [spread_next(): return paired.reshape(layout)]
  transfers between devices with their start and end apart: 13 -> 9, of which waited for: 8 -> 6; matrix products, arithmetic and copies ran while one was open for 0% -> 1% of each run, Pallas kernels for 27% -> 20%
where the time goes in v2:
time: 188 us
  blocking collectives  72.3 us (38%)
  Pallas kernels  60.2 us (32%)
  waiting for transfers between devices  27.5 us (15%)
  starting transfers between devices  20.5 us (11%)
  local copies, waits for them, and re-layouts  3.88 us (2%)
  other arithmetic  2.58 us (1%)
    all_gather x1, blocking collectives, on_device(): top_all = lax.all_gather(top_charge, ('gx', 'gy'), axis=0, tiled=False)  72.3 us
    pallas_call x2, Pallas kernels, cutoff(): pl.pallas_call(functools.partial(cutoff_kernel, tall), out_shape=jax.Shap...  47.5 us
    all_to_all x1, waiting for transfers between devices, fine_charges(): lax.all_to_all(outgoing, ('gx', 'gy'), split_axis=0, concat_axis=0, tiled...  16.9 us
    ppermute x4, starting transfers between devices, extended_2(): lax.ppermute(lax.slice_in_dim(block, 0, high_width, axis=dim), axis, back...  7.32 us
    all_to_all x1, starting transfers between devices, fine_charges(): lax.all_to_all(outgoing, ('gx', 'gy'), split_axis=0, concat_axis=0, tiled...  7.3 us
    ppermute x4, waiting for transfers between devices, extended_2(): lax.ppermute(lax.slice_in_dim(block, block.shape[dim] - low_width, None,...  7.06 us
    pallas_call x1, Pallas kernels, on_device(): pl.pallas_call(finish_kernel, out_shape=jax.ShapeDtypeStruct((CX, CY, NZ)...  6.2 us
    ppermute x4, starting transfers between devices, extended_2(): lax.ppermute(lax.slice_in_dim(block, block.shape[dim] - low_width, None,...  5.9 us
  transfers between devices with their start and end apart: 9, of which 6 were waited for; matrix products, arithmetic and copies ran while one was open for 1% of the time, Pallas kernels for 20%

profile of v2, /device:TPU:0, one launch (start us, length us, event | category | flops | bytes accessed | tf_op | source)
XLA Modules:
  0.0 188.0 jit_solution(15469121469463359709)
XLA Ops:
  0.7 0.7 fusion.48
  1.4 1.0 copy-done.2
  2.4 3.4 %shard_map.73 = f32[32,40,128]{2,1,0:T(8,128)} custom-call(s32[1]{0:T(128)S(6)} %copy.8.count_ref, s32[1,1024]{1,0:T(1,128)S(1)} %bitcast.5, s32[1,1024]{1,0:T(1,128)S(1)} %bitcast.4, f32[1024,128]{1,0:T(8,128)S(1)} %copy-done.2), custom_call_target="tpu_custom_call" | custom-call | tf_op jit(solution)/shard_map/pallas_call | solution.py:315
  5.8 7.3 %all-to-all-start = ((f32[32,40,128]{2,1,0:T(8,128)}), f32[32,40,128]{2,1,0:T(8,128)S(1)}, u32[]{:S(2)}, u32[]{:S(2)}) async-start(f32[32,40,128]{2,1,0:T(8,128)} %shard_map.73), calls=%async_computation | async-start | bytes 1310720 | tf_op jit(solution)/shard_map/all_to_all | solution.py:323
  13.2 16.9 %all-to-all-done.arrived_ref = f32[32,40,128]{2,1,0:T(8,128)S(1)} async-done(((f32[32,40,128]{2,1,0:T(8,128)}), f32[32,40,128]{2,1,0:T(8,128)S(1)}, u32[]{:S(2)}, u32[]{:S(2)}) %all-to-all-start) | async-done | bytes 655392 | tf_op jit(solution)/shard_map/all_to_all | solution.py:323
  30.1 0.1 convert_element_type.40.ids_ref
  30.2 2.3 %shard_map.74 = f32[24,32,256]{2,1,0:T(8,128)S(1)} custom-call(s32[1,1024]{1,0:T(1,128)S(1)} %convert_element_type.40.ids_ref, f32[32,40,128]{2,1,0:T(8,128)S(1)} %all-to-all-done.arrived_ref), custom_call_target="tpu_custom_call" | custom-call | tf_op jit(solution)/shard_map/pallas_call | solution.py:325
  32.6 1.4 collective-permute-start
  34.0 1.2 collective-permute-start.1
  35.3 1.0 fusion.3
  36.2 1.3 collective-permute-done
  37.6 3.9 %collective-permute-start.2 = (f32[4,40,256]{2,1,0:T(8,128)S(1)}, f32[4,40,256]{2,1,0:T(8,128)S(1)}, u32[]{:S(2)}, u32[]{:S(2)}) collective-permute-start(f32[4,40,256]{2,1,0:T(8,128)S(1)} %get-tuple-element.5), channel_id=1, source_target_pairs={{0,1},{1,2},{2,3},{3,0},{4,5},{5,6},{6,7},{7,4},{8,9},{9,10},{10,1... | collective-permute-start | bytes 491528 | tf_op jit(solution)/shard_map/ppermute | solution.py:193
  41.5 0.4 divide_exponential_fusion.plane_ref
  42.0 4.7 %collective-permute-done.2 = f32[4,40,256]{2,1,0:T(8,128)S(1)} collective-permute-done((f32[4,40,256]{2,1,0:T(8,128)S(1)}, f32[4,40,256]{2,1,0:T(8,128)S(1)}, u32[]{:S(2)}, u32[]{:S(2)}) %collective-permute-start.2) | collective-permute-done | bytes 163872 | tf_op jit(solution)/shard_map/ppermute | solution.py:193
  46.7 3.4 %collective-permute-done.3 = f32[4,40,256]{2,1,0:T(8,128)S(1)} collective-permute-done((f32[4,40,256]{2,1,0:T(8,128)S(1)}, f32[4,40,256]{2,1,0:T(8,128)S(1)}, u32[]{:S(2)}, u32[]{:S(2)}) %collective-permute-start.3) | collective-permute-done | bytes 163872 | tf_op jit(solution)/shard_map/ppermute | solution.py:196
  50.0 0.1 pad_maximum_fusion.padded_ref
  50.2 0.5 shard_map.75
  50.7 1.1 copy-done
  51.9 2.6 %collective-permute-start.5 = (f32[12,5,128]{2,1,0:T(8,128)S(1)}, f32[12,5,128]{2,1,0:T(8,128)S(1)}, u32[]{:S(2)}, u32[]{:S(2)}) collective-permute-start(f32[12,5,128]{2,1,0:T(8,128)S(1)} %slice.40), channel_id=1, source_target_pairs={{4,0},{8,4},{12,8},{16,12},{20,16},{24,20},{28,24},{0,28},{5,1},{9... | collective-permute-start | bytes 92168 | tf_op jit(solution)/shard_map/ppermute | solution.py:196
  54.5 0.1 fusion.15.along_ref
  54.6 0.1 reshape.231.kernel_ref
  54.8 0.1 reshape.230.kernel_ref
  54.9 1.1 collective-permute-done.4
  56.0 0.2 collective-permute-done.5
  56.3 0.5 collective-permute-start.6
  56.8 3.4 %collective-permute-start.7 = (f32[5,25,128]{2,1,0:T(8,128)S(1)}, f32[5,25,128]{2,1,0:T(8,128)S(1)}, u32[]{:S(2)}, u32[]{:S(2)}) collective-permute-start(f32[5,25,128]{2,1,0:T(8,128)S(1)} %pad_maximum_fusion.4), channel_id=1, source_target_pairs={{1,0},{2,1},{3,2},{0,3},{5,4},{6,5},{7,6},{4,7},{9,8},{10,9},{11,1... | collective-permute-start | bytes 192008 | tf_op jit(solution)/shard_map/ppermute | solution.py:196
  60.2 1.3 copy-done.1
  61.5 36.8 %shard_map.78.fine_ref = f32[24,32,256]{2,1,0:T(8,128)S(1)} custom-call(f32[729]{0:T(1024)S(1)} %reshape.231.kernel_ref, f32[32,40,256]{2,1,0:T(8,128)S(1)} %copy-done.1), custom_call_target="tpu_custom_call" | custom-call | flops 24461180928 | bytes 1572864 | tf_op jit(solution)/shard_map/pallas_call | solution.py:168
  98.4 0.3 shard_map.76
  98.8 10.7 %shard_map.77.mid_ref = f32[13,32,128]{2,1,0:T(8,128)S(1)} custom-call(f32[729]{0:T(1024)S(1)} %reshape.230.kernel_ref, f32[21,40,128]{2,1,0:T(8,128)S(1)} %select_maximum_fusion.padded_ref), custom_call_target="tpu_custom_call" | custom-call | flops 3312451584 | bytes 425984 | tf_op jit(solution)/shard_map/pallas_call | solution.py:168
  109.4 72.3 %all-gather = f32[192,8,64]{2,1,0:T(8,128)S(1)} all-gather(f32[6,8,64]{2,1,0:T(8,128)S(1)} %shard_map.76), channel_id=2, replica_groups=mesh['gx'=8,'gy'=4] {'gx','gy'}, dimensions={0}, use_global_device_ids=true | all-gather | bytes 405504 | tf_op jit(solution)/shard_map/all_gather | solution.py:346
  181.8 6.2 %shard_map.79 = f32[32,24,256]{2,1,0:T(8,128)} custom-call(f32[4,112,1536]{2,1,0:T(8,128)S(1)} %divide_exponential_fusion.plane_ref, f32[4,64,64]{2,1,0:T(8,128)S(1)} %fusion.15.along_ref, f32[32,6,8,64]{3,2,1,0:T(8,128)S(1)} %bitcast.3, f32[13,32,128]{2,1,0:T(8,128)S(1)} %shard_map.77.mid_ref, f32[24,32,256]{2,1,0:T(8,128)S(1)} %shard_map.78.fine_ref), custom_call_target="tpu_custom_call" | custom-call | tf_op jit(solution)/shard_map/pallas_call | solution.py:349
  (28 shorter events, 0.4 us)
Async XLA Ops:
  1.4 1.0 copy-start.2
  5.8 24.2 %all-to-all-start = ((f32[32,40,128]{2,1,0:T(8,128)}), f32[32,40,128]{2,1,0:T(8,128)S(1)}, u32[]{:S(2)}, u32[]{:S(2)}) async-start(f32[32,40,128]{2,1,0:T(8,128)} %shard_map.73), calls=%async_computation | async-start | bytes 1310720 | tf_op jit(solution)/shard_map/all_to_all | solution.py:323
  13.2 23.1 %copy-start.6 = (f32[4]{0:T(128)S(1)}, f32[4]{0:T(128)}, u32[]{:S(2)}) copy-start(f32[4]{0:T(128)} %param.13) | copy-start | bytes 52
  32.6 5.0 %collective-permute-start = (f32[24,4,256]{2,1,0:T(4,128)S(1)}, f32[24,4,256]{2,1,0:T(4,128)S(1)}, u32[]{:S(2)}, u32[]{:S(2)}) collective-permute-start(f32[24,4,256]{2,1,0:T(4,128)S(1)} %get-tuple-element.7), channel_id=1, source_target_pairs={{0,4},{4,8},{8,12},{12,16},{16,20},{20,24},{24,28},{28,0},{1,5},{5... | collective-permute-start | bytes 294920 | tf_op jit(solution)/shard_map/ppermute | solution.py:193
  34.0 3.5 %collective-permute-start.1 = (f32[24,4,256]{2,1,0:T(4,128)S(1)}, f32[24,4,256]{2,1,0:T(4,128)S(1)}, u32[]{:S(2)}, u32[]{:S(2)}) collective-permute-start(f32[24,4,256]{2,1,0:T(4,128)S(1)} %get-tuple-element.8), channel_id=1, source_target_pairs={{4,0},{8,4},{12,8},{16,12},{20,16},{24,20},{28,24},{0,28},{5,1},{9... | collective-permute-start | bytes 294920 | tf_op jit(solution)/shard_map/ppermute | solution.py:196
  37.6 9.1 %collective-permute-start.2 = (f32[4,40,256]{2,1,0:T(8,128)S(1)}, f32[4,40,256]{2,1,0:T(8,128)S(1)}, u32[]{:S(2)}, u32[]{:S(2)}) collective-permute-start(f32[4,40,256]{2,1,0:T(8,128)S(1)} %get-tuple-element.5), channel_id=1, source_target_pairs={{0,1},{1,2},{2,3},{3,0},{4,5},{5,6},{6,7},{7,4},{8,9},{9,10},{10,1... | collective-permute-start | bytes 491528 | tf_op jit(solution)/shard_map/ppermute | solution.py:193
  41.5 8.5 %collective-permute-start.3 = (f32[4,40,256]{2,1,0:T(8,128)S(1)}, f32[4,40,256]{2,1,0:T(8,128)S(1)}, u32[]{:S(2)}, u32[]{:S(2)}) collective-permute-start(f32[4,40,256]{2,1,0:T(8,128)S(1)} %get-tuple-element.6), channel_id=1, source_target_pairs={{1,0},{2,1},{3,2},{0,3},{5,4},{6,5},{7,6},{4,7},{9,8},{10,9},{11,1... | collective-permute-start | bytes 491528 | tf_op jit(solution)/shard_map/ppermute | solution.py:196
  50.2 4.3 %copy-start.5 = (f32[4]{0:T(128)S(1)}, f32[4]{0:T(128)}, u32[]{:S(2)}) copy-start(f32[4]{0:T(128)} %param.12) | copy-start | bytes 52
  50.2 4.4 %copy-start.3 = (f32[9,9,9]{2,1,0:T(8,128)S(1)}, f32[9,9,9]{2,1,0:T(8,128)}, u32[]{:S(2)}) copy-start(f32[9,9,9]{2,1,0:T(8,128)} %param.10) | copy-start | bytes 8752
  50.2 4.6 %copy-start.4 = (f32[9,9,9]{2,1,0:T(8,128)S(1)}, f32[9,9,9]{2,1,0:T(8,128)}, u32[]{:S(2)}) copy-start(f32[9,9,9]{2,1,0:T(8,128)} %param.11) | copy-start | bytes 8752
  50.7 1.1 copy-start
  51.8 4.2 %collective-permute-start.4 = (f32[12,4,128]{2,1,0:T(4,128)S(1)}, f32[12,4,128]{2,1,0:T(4,128)S(1)}, u32[]{:S(2)}, u32[]{:S(2)}) collective-permute-start(f32[12,4,128]{2,1,0:T(4,128)S(1)} %slice.39), channel_id=1, source_target_pairs={{0,4},{4,8},{8,12},{12,16},{16,20},{20,24},{24,28},{28,0},{1,5},{5... | collective-permute-start | bytes 73736 | tf_op jit(solution)/shard_map/ppermute | solution.py:193
  51.9 4.4 %collective-permute-start.5 = (f32[12,5,128]{2,1,0:T(8,128)S(1)}, f32[12,5,128]{2,1,0:T(8,128)S(1)}, u32[]{:S(2)}, u32[]{:S(2)}) collective-permute-start(f32[12,5,128]{2,1,0:T(8,128)S(1)} %slice.40), channel_id=1, source_target_pairs={{4,0},{8,4},{12,8},{16,12},{20,16},{24,20},{28,24},{0,28},{5,1},{9... | collective-permute-start | bytes 92168 | tf_op jit(solution)/shard_map/ppermute | solution.py:196
  56.3 42.1 %collective-permute-start.6 = (f32[4,25,128]{2,1,0:T(8,128)S(1)}, f32[4,25,128]{2,1,0:T(8,128)S(1)}, u32[]{:S(2)}, u32[]{:S(2)}) collective-permute-start(f32[4,25,128]{2,1,0:T(8,128)S(1)} %pad_maximum_fusion.6), channel_id=1, source_target_pairs={{0,1},{1,2},{2,3},{3,0},{4,5},{5,6},{6,7},{7,4},{8,9},{9,10},{10,1... | collective-permute-start | bytes 153608 | tf_op jit(solution)/shard_map/ppermute | solution.py:193
  56.8 41.6 %collective-permute-start.7 = (f32[5,25,128]{2,1,0:T(8,128)S(1)}, f32[5,25,128]{2,1,0:T(8,128)S(1)}, u32[]{:S(2)}, u32[]{:S(2)}) collective-permute-start(f32[5,25,128]{2,1,0:T(8,128)S(1)} %pad_maximum_fusion.4), channel_id=1, source_target_pairs={{1,0},{2,1},{3,2},{0,3},{5,4},{6,5},{7,6},{4,7},{9,8},{10,9},{11,1... | collective-permute-start | bytes 192008 | tf_op jit(solution)/shard_map/ppermute | solution.py:196
  60.2 1.3 copy-start.1

commit v3 on v2

--- a/solution.py
+++ b/solution.py
@@ -285,8 +285,8 @@
     top_x, top_y, depth = CX // 4, CY // 4, NZ // 4
     cols = jnp.arange(size_x * size_y * top_x * top_y, dtype=jnp.int32)
     owner = cols // (top_x * top_y)
-    col_x = owner // size_y * top_x + cols % top_x
-    col_y = owner % size_y * top_y + cols // top_x % top_y
+    col_x = owner % size_x * top_x + cols % top_x
+    col_y = owner // size_x * top_y + cols // top_x % top_y
     rows = jnp.arange((top_y + 1) * 16, dtype=jnp.int32)
     row_x = lax.axis_index("gx") * top_x + rows % 16
     row_y = lax.axis_index("gy") * top_y + rows // 16
@@ -343,7 +343,8 @@
     spare = CX + 2 * RADIUS - mid_padded.shape[1]
     mid_padded = jnp.pad(mid_padded, ((0, 0), (0, spare), (0, 0)))
     top_charge = restrict(mid_padded, CY // 4, CX // 4)
-    top_all = lax.all_gather(top_charge, ("gx", "gy"), axis=0, tiled=False)
+    top_all = lax.all_gather(top_charge[None], "gx", axis=0, tiled=True)
+    top_all = lax.all_gather(top_all, "gy", axis=0, tiled=True)
     mid_cut = cutoff(mid_padded, mid_kernel, CY // 2 + 1)
     fine_cut = cutoff(fine_padded, near_kernel, 8)
     return pl.pallas_call(

time: 188 us -> 143 us (0.76)
  blocking collectives: 72.3 us -> 27 us
    all_gather x1 -> x2, blocking collectives: 72.3 us -> 27 us  [the longest x1 17.7 us: on_device(): top_all = lax.all_gather(top_all, 'gy', axis=0, tiled=True)]
  transfers between devices with their start and end apart: 9 -> 9, of which waited for: 6 -> 6; matrix products, arithmetic and copies ran while one was open for 1% -> 1% of each run, Pallas kernels for 20% -> 26%
where the time goes in v3:
time: 143 us
  Pallas kernels  60.2 us (42%)
  waiting for transfers between devices  27.5 us (19%)
  blocking collectives  27 us (19%)
  starting transfers between devices  20.5 us (14%)
  local copies, waits for them, and re-layouts  3.88 us (3%)
  other arithmetic  2.58 us (2%)
    pallas_call x2, Pallas kernels, cutoff(): pl.pallas_call(functools.partial(cutoff_kernel, tall), out_shape=jax.Shap...  47.5 us
    all_gather x1, blocking collectives, on_device(): top_all = lax.all_gather(top_all, 'gy', axis=0, tiled=True)  17.7 us
    all_to_all x1, waiting for transfers between devices, fine_charges(): lax.all_to_all(outgoing, ('gx', 'gy'), split_axis=0, concat_axis=0, tiled...  16.9 us
    all_gather x1, blocking collectives, on_device(): top_all = lax.all_gather(top_charge[None], 'gx', axis=0, tiled=True)  9.25 us
    ppermute x4, starting transfers between devices, extended_2(): lax.ppermute(lax.slice_in_dim(block, 0, high_width, axis=dim), axis, back...  7.32 us
    all_to_all x1, starting transfers between devices, fine_charges(): lax.all_to_all(outgoing, ('gx', 'gy'), split_axis=0, concat_axis=0, tiled...  7.3 us
    ppermute x4, waiting for transfers between devices, extended_2(): lax.ppermute(lax.slice_in_dim(block, block.shape[dim] - low_width, None,...  7.06 us
    pallas_call x1, Pallas kernels, on_device(): pl.pallas_call(finish_kernel, out_shape=jax.ShapeDtypeStruct((CX, CY, NZ)...  6.2 us
  transfers between devices with their start and end apart: 9, of which 6 were waited for; matrix products, arithmetic and copies ran while one was open for 1% of the time, Pallas kernels for 26%

profile of v3, /device:TPU:0, one launch (start us, length us, event | category | flops | bytes accessed | tf_op | source)
XLA Modules:
  0.0 142.6 jit_solution(9757231171077329551)
XLA Ops:
  0.7 0.7 fusion.48
  1.4 1.0 copy-done.2
  2.4 3.4 %shard_map.73 = f32[32,40,128]{2,1,0:T(8,128)} custom-call(s32[1]{0:T(128)S(6)} %copy.8.count_ref, s32[1,1024]{1,0:T(1,128)S(1)} %bitcast.4, s32[1,1024]{1,0:T(1,128)S(1)} %bitcast.3, f32[1024,128]{1,0:T(8,128)S(1)} %copy-done.2), custom_call_target="tpu_custom_call" | custom-call | tf_op jit(solution)/shard_map/pallas_call | solution.py:315
  5.8 7.3 %all-to-all-start = ((f32[32,40,128]{2,1,0:T(8,128)}), f32[32,40,128]{2,1,0:T(8,128)S(1)}, u32[]{:S(2)}, u32[]{:S(2)}) async-start(f32[32,40,128]{2,1,0:T(8,128)} %shard_map.73), calls=%async_computation | async-start | bytes 1310720 | tf_op jit(solution)/shard_map/all_to_all | solution.py:323
  13.2 16.9 %all-to-all-done.arrived_ref = f32[32,40,128]{2,1,0:T(8,128)S(1)} async-done(((f32[32,40,128]{2,1,0:T(8,128)}), f32[32,40,128]{2,1,0:T(8,128)S(1)}, u32[]{:S(2)}, u32[]{:S(2)}) %all-to-all-start) | async-done | bytes 655392 | tf_op jit(solution)/shard_map/all_to_all | solution.py:323
  30.2 2.3 %shard_map.74 = f32[24,32,256]{2,1,0:T(8,128)S(1)} custom-call(s32[1,1024]{1,0:T(1,128)S(1)} %convert_element_type.40.ids_ref, f32[32,40,128]{2,1,0:T(8,128)S(1)} %all-to-all-done.arrived_ref), custom_call_target="tpu_custom_call" | custom-call | tf_op jit(solution)/shard_map/pallas_call | solution.py:325
  32.6 1.4 %collective-permute-start = (f32[24,4,256]{2,1,0:T(4,128)S(1)}, f32[24,4,256]{2,1,0:T(4,128)S(1)}, u32[]{:S(2)}, u32[]{:S(2)}) collective-permute-start(f32[24,4,256]{2,1,0:T(4,128)S(1)} %get-tuple-element.7), channel_id=1, source_target_pairs={{0,4},{4,8},{8,12},{12,16},{16,20},{20,24},{24,28},{28,0},{1,5},{5... | collective-permute-start | bytes 294920 | tf_op jit(solution)/shard_map/ppermute | solution.py:193
  34.0 1.2 collective-permute-start.1
  35.3 1.0 fusion.3
  36.2 1.3 collective-permute-done
  37.6 3.9 %collective-permute-start.2 = (f32[4,40,256]{2,1,0:T(8,128)S(1)}, f32[4,40,256]{2,1,0:T(8,128)S(1)}, u32[]{:S(2)}, u32[]{:S(2)}) collective-permute-start(f32[4,40,256]{2,1,0:T(8,128)S(1)} %get-tuple-element.5), channel_id=1, source_target_pairs={{0,1},{1,2},{2,3},{3,0},{4,5},{5,6},{6,7},{7,4},{8,9},{9,10},{10,1... | collective-permute-start | bytes 491528 | tf_op jit(solution)/shard_map/ppermute | solution.py:193
  41.5 0.4 divide_exponential_fusion.plane_ref
  42.0 4.7 %collective-permute-done.2 = f32[4,40,256]{2,1,0:T(8,128)S(1)} collective-permute-done((f32[4,40,256]{2,1,0:T(8,128)S(1)}, f32[4,40,256]{2,1,0:T(8,128)S(1)}, u32[]{:S(2)}, u32[]{:S(2)}) %collective-permute-start.2) | collective-permute-done | bytes 163872 | tf_op jit(solution)/shard_map/ppermute | solution.py:193
  46.7 3.4 %collective-permute-done.3 = f32[4,40,256]{2,1,0:T(8,128)S(1)} collective-permute-done((f32[4,40,256]{2,1,0:T(8,128)S(1)}, f32[4,40,256]{2,1,0:T(8,128)S(1)}, u32[]{:S(2)}, u32[]{:S(2)}) %collective-permute-start.3) | collective-permute-done | bytes 163872 | tf_op jit(solution)/shard_map/ppermute | solution.py:196
  50.0 0.1 pad_maximum_fusion.padded_ref
  50.2 0.5 shard_map.75
  50.7 1.1 copy-done
  51.9 2.6 %collective-permute-start.5 = (f32[12,5,128]{2,1,0:T(8,128)S(1)}, f32[12,5,128]{2,1,0:T(8,128)S(1)}, u32[]{:S(2)}, u32[]{:S(2)}) collective-permute-start(f32[12,5,128]{2,1,0:T(8,128)S(1)} %slice.40), channel_id=1, source_target_pairs={{4,0},{8,4},{12,8},{16,12},{20,16},{24,20},{28,24},{0,28},{5,1},{9... | collective-permute-start | bytes 92168 | tf_op jit(solution)/shard_map/ppermute | solution.py:196
  54.5 0.1 fusion.15.along_ref
  54.6 0.1 reshape.231.kernel_ref
  54.8 0.1 reshape.230.kernel_ref
  54.9 1.1 collective-permute-done.4
  56.0 0.2 collective-permute-done.5
  56.3 0.5 collective-permute-start.6
  56.8 3.4 %collective-permute-start.7 = (f32[5,25,128]{2,1,0:T(8,128)S(1)}, f32[5,25,128]{2,1,0:T(8,128)S(1)}, u32[]{:S(2)}, u32[]{:S(2)}) collective-permute-start(f32[5,25,128]{2,1,0:T(8,128)S(1)} %pad_maximum_fusion.4), channel_id=1, source_target_pairs={{1,0},{2,1},{3,2},{0,3},{5,4},{6,5},{7,6},{4,7},{9,8},{10,9},{11,1... | collective-permute-start | bytes 192008 | tf_op jit(solution)/shard_map/ppermute | solution.py:196
  60.2 1.3 copy-done.1
  61.5 36.8 %shard_map.78.fine_ref = f32[24,32,256]{2,1,0:T(8,128)S(1)} custom-call(f32[729]{0:T(1024)S(1)} %reshape.231.kernel_ref, f32[32,40,256]{2,1,0:T(8,128)S(1)} %copy-done.1), custom_call_target="tpu_custom_call" | custom-call | flops 24461180928 | bytes 1572864 | tf_op jit(solution)/shard_map/pallas_call | solution.py:168
  98.4 0.3 shard_map.76
  98.8 10.7 %shard_map.77.mid_ref = f32[13,32,128]{2,1,0:T(8,128)S(1)} custom-call(f32[729]{0:T(1024)S(1)} %reshape.230.kernel_ref, f32[21,40,128]{2,1,0:T(8,128)S(1)} %select_maximum_fusion.padded_ref), custom_call_target="tpu_custom_call" | custom-call | flops 3312451584 | bytes 425984 | tf_op jit(solution)/shard_map/pallas_call | solution.py:168
  109.4 9.3 %all-gather = f32[48,8,64]{2,1,0:T(8,128)S(1)} all-gather(f32[6,8,64]{2,1,0:T(8,128)S(1)} %shard_map.76), channel_id=2, replica_groups=mesh['gx'=8,'gy'=4] {'gx'}, dimensions={0}, use_global_device_ids=true | all-gather | bytes 110592 | tf_op jit(solution)/shard_map/all_gather | solution.py:346
  118.7 17.7 %all_gather.7.top_ref = f32[32,6,8,64]{3,2,1,0:T(8,128)S(1)} all-gather(f32[8,6,8,64]{3,2,1,0:T(8,128)S(1)} %bitcast.5), channel_id=1, replica_groups=mesh['gx'=8,'gy'=4] {'gy'}, dimensions={0}, use_global_device_ids=true | all-gather | bytes 491520 | tf_op jit(solution)/shard_map/all_gather | solution.py:347
  136.4 6.2 %shard_map.79 = f32[32,24,256]{2,1,0:T(8,128)} custom-call(f32[4,112,1536]{2,1,0:T(8,128)S(1)} %divide_exponential_fusion.plane_ref, f32[4,64,64]{2,1,0:T(8,128)S(1)} %fusion.15.along_ref, f32[32,6,8,64]{3,2,1,0:T(8,128)S(1)} %all_gather.7.top_ref, f32[13,32,128]{2,1,0:T(8,128)S(1)} %shard_map.77.mid_ref, f32[24,32,256]{2,1,0:T(8,128)S(1)} %shard_map.78.fine_ref), custom_call_target="tpu_custom_call" | custom-call | tf_op jit(solution)/shard_map/pallas_call | solution.py:350
  (29 shorter events, 0.5 us)
Async XLA Ops:
  1.4 1.0 copy-start.2
  5.8 24.2 %all-to-all-start = ((f32[32,40,128]{2,1,0:T(8,128)}), f32[32,40,128]{2,1,0:T(8,128)S(1)}, u32[]{:S(2)}, u32[]{:S(2)}) async-start(f32[32,40,128]{2,1,0:T(8,128)} %shard_map.73), calls=%async_computation | async-start | bytes 1310720 | tf_op jit(solution)/shard_map/all_to_all | solution.py:323
  13.2 23.1 %copy-start.6 = (f32[4]{0:T(128)S(1)}, f32[4]{0:T(128)}, u32[]{:S(2)}) copy-start(f32[4]{0:T(128)} %param.13) | copy-start | bytes 52
  32.6 5.0 %collective-permute-start = (f32[24,4,256]{2,1,0:T(4,128)S(1)}, f32[24,4,256]{2,1,0:T(4,128)S(1)}, u32[]{:S(2)}, u32[]{:S(2)}) collective-permute-start(f32[24,4,256]{2,1,0:T(4,128)S(1)} %get-tuple-element.7), channel_id=1, source_target_pairs={{0,4},{4,8},{8,12},{12,16},{16,20},{20,24},{24,28},{28,0},{1,5},{5... | collective-permute-start | bytes 294920 | tf_op jit(solution)/shard_map/ppermute | solution.py:193
  34.0 3.5 %collective-permute-start.1 = (f32[24,4,256]{2,1,0:T(4,128)S(1)}, f32[24,4,256]{2,1,0:T(4,128)S(1)}, u32[]{:S(2)}, u32[]{:S(2)}) collective-permute-start(f32[24,4,256]{2,1,0:T(4,128)S(1)} %get-tuple-element.8), channel_id=1, source_target_pairs={{4,0},{8,4},{12,8},{16,12},{20,16},{24,20},{28,24},{0,28},{5,1},{9... | collective-permute-start | bytes 294920 | tf_op jit(solution)/shard_map/ppermute | solution.py:196
  37.6 9.1 %collective-permute-start.2 = (f32[4,40,256]{2,1,0:T(8,128)S(1)}, f32[4,40,256]{2,1,0:T(8,128)S(1)}, u32[]{:S(2)}, u32[]{:S(2)}) collective-permute-start(f32[4,40,256]{2,1,0:T(8,128)S(1)} %get-tuple-element.5), channel_id=1, source_target_pairs={{0,1},{1,2},{2,3},{3,0},{4,5},{5,6},{6,7},{7,4},{8,9},{9,10},{10,1... | collective-permute-start | bytes 491528 | tf_op jit(solution)/shard_map/ppermute | solution.py:193
  41.5 8.5 %collective-permute-start.3 = (f32[4,40,256]{2,1,0:T(8,128)S(1)}, f32[4,40,256]{2,1,0:T(8,128)S(1)}, u32[]{:S(2)}, u32[]{:S(2)}) collective-permute-start(f32[4,40,256]{2,1,0:T(8,128)S(1)} %get-tuple-element.6), channel_id=1, source_target_pairs={{1,0},{2,1},{3,2},{0,3},{5,4},{6,5},{7,6},{4,7},{9,8},{10,9},{11,1... | collective-permute-start | bytes 491528 | tf_op jit(solution)/shard_map/ppermute | solution.py:196
  50.2 4.3 %copy-start.5 = (f32[4]{0:T(128)S(1)}, f32[4]{0:T(128)}, u32[]{:S(2)}) copy-start(f32[4]{0:T(128)} %param.12) | copy-start | bytes 52
  50.2 4.4 %copy-start.3 = (f32[9,9,9]{2,1,0:T(8,128)S(1)}, f32[9,9,9]{2,1,0:T(8,128)}, u32[]{:S(2)}) copy-start(f32[9,9,9]{2,1,0:T(8,128)} %param.10) | copy-start | bytes 8752
  50.2 4.6 %copy-start.4 = (f32[9,9,9]{2,1,0:T(8,128)S(1)}, f32[9,9,9]{2,1,0:T(8,128)}, u32[]{:S(2)}) copy-start(f32[9,9,9]{2,1,0:T(8,128)} %param.11) | copy-start | bytes 8752
  50.7 1.1 copy-start
  51.8 4.2 %collective-permute-start.4 = (f32[12,4,128]{2,1,0:T(4,128)S(1)}, f32[12,4,128]{2,1,0:T(4,128)S(1)}, u32[]{:S(2)}, u32[]{:S(2)}) collective-permute-start(f32[12,4,128]{2,1,0:T(4,128)S(1)} %slice.39), channel_id=1, source_target_pairs={{0,4},{4,8},{8,12},{12,16},{16,20},{20,24},{24,28},{28,0},{1,5},{5... | collective-permute-start | bytes 73736 | tf_op jit(solution)/shard_map/ppermute | solution.py:193
  51.9 4.4 %collective-permute-start.5 = (f32[12,5,128]{2,1,0:T(8,128)S(1)}, f32[12,5,128]{2,1,0:T(8,128)S(1)}, u32[]{:S(2)}, u32[]{:S(2)}) collective-permute-start(f32[12,5,128]{2,1,0:T(8,128)S(1)} %slice.40), channel_id=1, source_target_pairs={{4,0},{8,4},{12,8},{16,12},{20,16},{24,20},{28,24},{0,28},{5,1},{9... | collective-permute-start | bytes 92168 | tf_op jit(solution)/shard_map/ppermute | solution.py:196
  56.3 42.1 %collective-permute-start.6 = (f32[4,25,128]{2,1,0:T(8,128)S(1)}, f32[4,25,128]{2,1,0:T(8,128)S(1)}, u32[]{:S(2)}, u32[]{:S(2)}) collective-permute-start(f32[4,25,128]{2,1,0:T(8,128)S(1)} %pad_maximum_fusion.6), channel_id=1, source_target_pairs={{0,1},{1,2},{2,3},{3,0},{4,5},{5,6},{6,7},{7,4},{8,9},{9,10},{10,1... | collective-permute-start | bytes 153608 | tf_op jit(solution)/shard_map/ppermute | solution.py:193
  56.8 41.6 %collective-permute-start.7 = (f32[5,25,128]{2,1,0:T(8,128)S(1)}, f32[5,25,128]{2,1,0:T(8,128)S(1)}, u32[]{:S(2)}, u32[]{:S(2)}) collective-permute-start(f32[5,25,128]{2,1,0:T(8,128)S(1)} %pad_maximum_fusion.4), channel_id=1, source_target_pairs={{1,0},{2,1},{3,2},{0,3},{5,4},{6,5},{7,6},{4,7},{9,8},{10,9},{11,1... | collective-permute-start | bytes 192008 | tf_op jit(solution)/shard_map/ppermute | solution.py:196
  60.2 1.3 copy-start.1
